TPU v7x, 256 devices: a whole 4x4x8 slice. The times are simulated.
256 devices in a mesh: segment: 4 (over x), expert: 64 (over z, y, core).
Axes of the slice: x: 4, y: 4, z: 8, core: 2. Of those that a mesh axis runs over, the one named last changes fastest.
Arguments:
- tokens: bfloat16 [2, 4096, 3584], P(None, 'expert'), may hold values from -6 to 6
- norm_gain: float32 [4, 2, 3584], P('segment'), may hold values from 0.1 to 1.9
- gate_weight: bfloat16 [4, 2, 3584, 16384], P('segment', None, None, 'expert'), may hold values from -0.09375 to 0.09375
- up_weight: bfloat16 [4, 2, 3584, 16384], P('segment', None, None, 'expert'), may hold values from -0.09375 to 0.09375
- down_weight: bfloat16 [4, 2, 16384, 3584], P('segment', None, 'expert'), may hold values from -0.125 to 0.125
- expert_ids: int32 [4, 2, 2, 4096], P('segment', None, None, 'expert'), may hold values from 0 to 8, as said below
- gate_scale: float32 [4, 2, 2, 4096], P('segment', None, None, 'expert'), may hold values from 0.5 to 2
- depths: int32 [4], P('segment'), may hold values from 1 to 2, as said below
Outputs:
- section_out: bfloat16 [4, 2, 4096, 3584], P('segment', None, 'expert')
Inputs may be any that keep to these rules, and one draw needn't show every extreme that they name: `expert_ids`: 8 marks a token routed outside this layer's experts. In each aligned block of 64 tokens (one device's tokens of one section, layer and micro-batch) exactly 8 tokens name an expert below 8; no expert is named by more than 2 of them, and one by exactly 2. `depths`: at least one section applies 2 layers and at least one applies 1.
All inputs are finite; a program needn't handle non-finite values.
Results may differ from a plain program's by a relative error of at most 0.012.
Values may be sent and summed in bfloat16 or wider, within the bound.
A program may use at most 128 MiB of HBM per device.

v0:
```python
import jax
import jax.numpy as jnp
from jax import lax
from jax.sharding import PartitionSpec as P

GROUP = 8
LMAX = 2
MB = 2
TOK_DEV = 64
ROUTED = 8


def from_behind(value, axis, steps):
    count = lax.axis_size(axis)
    leading, last = (max(0, -steps), min(count, count - steps))
    return lax.ppermute(value, axis, [(source, source + steps) for source in range(leading, last)])


def moe_layer(state, gain, gate_w, up_w, down_w, routing, scaling, window_experts, capacity):
    widened = state.astype(jnp.float32)
    ratio = lax.rsqrt(jnp.mean(widened * widened, axis=-1, keepdims=True) + 1e-06)
    normed = (widened * ratio * gain).astype(jnp.bfloat16)
    width = state.shape[1]
    onehot = (routing[:, None] == jnp.arange(window_experts, dtype=jnp.int32)[None, :]).astype(
        jnp.int32
    )
    ranking = jnp.cumsum(onehot, axis=0) * onehot
    routed = routing < window_experts
    targets = jnp.where(routed, routing * capacity + jnp.sum(ranking, axis=1) - 1, -1)
    dispatch_table = (
        jnp.arange(window_experts * capacity, dtype=jnp.int32)[:, None] == targets[None, :]
    ).astype(jnp.bfloat16)
    packed = jnp.dot(dispatch_table, normed, preferred_element_type=jnp.float32).astype(
        jnp.bfloat16
    )
    spread = jnp.broadcast_to(
        packed.reshape(window_experts, 1, capacity, width), (window_experts, GROUP, capacity, width)
    ).reshape(window_experts * GROUP, capacity, width)
    received = lax.all_to_all(spread, "expert", split_axis=0, concat_axis=0, tiled=True)
    flattened = received.reshape(-1, width)
    gate_pre = jnp.dot(flattened, gate_w, preferred_element_type=jnp.float32)
    up_pre = jnp.dot(flattened, up_w, preferred_element_type=jnp.float32)
    hidden = (jax.nn.silu(gate_pre) * up_pre).astype(jnp.bfloat16)
    partial_value = jnp.dot(hidden, down_w, preferred_element_type=jnp.float32).astype(jnp.bfloat16)
    returned = lax.all_to_all(
        partial_value.reshape(received.shape), "expert", split_axis=0, concat_axis=0, tiled=True
    )
    summed = jnp.sum(
        returned.astype(jnp.float32).reshape(window_experts, GROUP, capacity, width), axis=1
    )
    summed = summed.reshape(window_experts * capacity, width)
    picked = jnp.take(summed, jnp.clip(targets, 0, window_experts * capacity - 1), axis=0)
    picked = jnp.where(routed[:, None], picked, jnp.zeros_like(picked))
    return (widened + scaling[:, None] * picked).astype(jnp.bfloat16)


def local(tokens, norm_gain, gate_weight, up_weight, down_weight, expert_ids, gate_scale, depths):
    segments = lax.axis_size("segment")
    members = lax.axis_size("expert")
    position = lax.axis_index("segment")
    window_experts = members // GROUP
    capacity = min(ROUTED, max(2, 3 * ROUTED // (2 * window_experts)))
    width = tokens.shape[2]
    pieces = MB
    row_count = MB * TOK_DEV // pieces
    routing_all = expert_ids[0]
    scaling_all = gate_scale[0]
    own_depth = depths[0]
    result = jnp.zeros((pieces, row_count, width), jnp.bfloat16)
    carried = jnp.zeros((row_count, width), jnp.bfloat16)
    for tick_idx in range(pieces + segments - 1):
        piece_now = tick_idx - position
        active = (piece_now >= 0) & (piece_now < pieces)
        current = jnp.clip(piece_now, 0, pieces - 1)
        entering = lax.dynamic_index_in_dim(tokens, current, 0, keepdims=False)
        state = jnp.where(position == 0, entering, carried)
        for layer_idx in range(LMAX):
            routing = lax.dynamic_index_in_dim(routing_all[layer_idx], current, 0, keepdims=False)
            scaling = lax.dynamic_index_in_dim(scaling_all[layer_idx], current, 0, keepdims=False)
            moved = moe_layer(
                state,
                norm_gain[0, layer_idx],
                gate_weight[0, layer_idx],
                up_weight[0, layer_idx],
                down_weight[0, layer_idx],
                routing,
                scaling,
                window_experts,
                capacity,
            )
            state = jnp.where(layer_idx < own_depth, moved, state)
        result = jnp.where(
            active, lax.dynamic_update_index_in_dim(result, state, current, 0), result
        )
        carried = from_behind(state, "segment", 1)
    return result.reshape(1, MB, TOK_DEV, width)


def solution(mesh):
    return jax.shard_map(
        local,
        mesh=mesh,
        in_specs=(
            P(None, "expert", None),
            P("segment", None, None),
            P("segment", None, None, "expert"),
            P("segment", None, None, "expert"),
            P("segment", None, "expert", None),
            P("segment", None, None, "expert"),
            P("segment", None, None, "expert"),
            P("segment"),
        ),
        out_specs=P("segment", None, "expert", None),
        check_vma=False,
    )
```

profile of v0, /device:TPU:6, one launch (start us, length us, event | category | flops | bytes accessed | tf_op | source)
XLA Modules:
  0.0 838.0 jit_solution(15716025161012888331)
XLA Ops:
  5.5 38.0 %all_to_all.100 = bf16[64,2,3584]{2,1,0:T(2,128)(2,1)S(1)} all-to-all(bf16[64,2,3584]{2,1,0:T(2,128)(2,1)S(1)} %bitcast.282), channel_id=1, replica_groups=mesh['segment'=4,'expert'=64] {'expert'}, dimensions={0} | all-to-all | bytes 1835008 | tf_op jit(solution)/shard_map/all_to_all | solution.py:39
  43.8 1.9 fusion.48
  45.7 3.2 convolution_convert_fusion.9
  50.3 5.7 all-to-all-start.1
  57.2 24.9 %all-to-all-done.1 = bf16[64,2,3584]{2,1,0:T(2,128)(2,1)S(1)} async-done(((bf16[64,2,3584]{2,1,0:T(2,128)(2,1)}), bf16[64,2,3584]{2,1,0:T(2,128)(2,1)S(1)}, u32[]{:S(2)}, u32[]{:S(2)}) %all-to-all-start.1) | async-done | bytes 917536 | tf_op jit(solution)/shard_map/all_to_all | solution.py:45
  85.4 31.6 %all_to_all.101 = bf16[64,2,3584]{2,1,0:T(2,128)(2,1)S(1)} all-to-all(bf16[64,2,3584]{2,1,0:T(2,128)(2,1)S(1)} %bitcast.283), channel_id=1, replica_groups=mesh['segment'=4,'expert'=64] {'expert'}, dimensions={0} | all-to-all | bytes 1835008 | tf_op jit(solution)/shard_map/all_to_all | solution.py:39
  117.3 1.9 fusion.23
  119.3 3.2 convolution_convert_fusion.8
  123.8 5.8 all-to-all-start.3
  130.3 25.4 %all-to-all-done.3 = bf16[64,2,3584]{2,1,0:T(2,128)(2,1)S(1)} async-done(((bf16[64,2,3584]{2,1,0:T(2,128)(2,1)}), bf16[64,2,3584]{2,1,0:T(2,128)(2,1)S(1)}, u32[]{:S(2)}, u32[]{:S(2)}) %all-to-all-start.3) | async-done | bytes 917536 | tf_op jit(solution)/shard_map/all_to_all | solution.py:45
  161.3 11.3 %collective-permute-done = bf16[64,3584]{1,0:T(8,128)(2,1)S(1)} collective-permute-done((bf16[64,3584]{1,0:T(8,128)(2,1)}, bf16[64,3584]{1,0:T(8,128)(2,1)S(1)}, u32[]{:S(2)}, u32[]{:S(2)}) %collective-permute-start) | collective-permute-done | bytes 458784 | tf_op jit(solution)/shard_map/ppermute | solution.py:16
  173.7 31.9 %all_to_all.102 = bf16[64,2,3584]{2,1,0:T(2,128)(2,1)S(1)} all-to-all(bf16[64,2,3584]{2,1,0:T(2,128)(2,1)S(1)} %bitcast.284), channel_id=1, replica_groups=mesh['segment'=4,'expert'=64] {'expert'}, dimensions={0} | all-to-all | bytes 1835008 | tf_op jit(solution)/shard_map/all_to_all | solution.py:39
  206.8 2.3 fusion.46
  209.1 4.2 convolution_convert_fusion.7
  213.3 3.1 reshape.594
  216.3 5.7 all-to-all-start.5
  222.0 26.1 %all-to-all-done.5 = bf16[64,2,3584]{2,1,0:T(2,128)(2,1)S(1)} async-done(((bf16[64,2,3584]{2,1,0:T(2,128)(2,1)}), bf16[64,2,3584]{2,1,0:T(2,128)(2,1)S(1)}, u32[]{:S(2)}, u32[]{:S(2)}) %all-to-all-start.5) | async-done | bytes 917536 | tf_op jit(solution)/shard_map/all_to_all | solution.py:45
  248.1 1.5 convert_reduce_fusion.7
  253.6 31.8 %all_to_all.103 = bf16[64,2,3584]{2,1,0:T(2,128)(2,1)S(1)} all-to-all(bf16[64,2,3584]{2,1,0:T(2,128)(2,1)S(1)} %bitcast.285), channel_id=1, replica_groups=mesh['segment'=4,'expert'=64] {'expert'}, dimensions={0} | all-to-all | bytes 1835008 | tf_op jit(solution)/shard_map/all_to_all | solution.py:39
  286.6 2.3 fusion.21
  288.9 4.2 convolution_convert_fusion.6
  293.1 3.1 reshape.600
  296.2 5.7 all-to-all-start.7
  301.9 26.0 %all-to-all-done.7 = bf16[64,2,3584]{2,1,0:T(2,128)(2,1)S(1)} async-done(((bf16[64,2,3584]{2,1,0:T(2,128)(2,1)}), bf16[64,2,3584]{2,1,0:T(2,128)(2,1)S(1)}, u32[]{:S(2)}, u32[]{:S(2)}) %all-to-all-start.7) | async-done | bytes 917536 | tf_op jit(solution)/shard_map/all_to_all | solution.py:45
  332.7 12.1 %collective-permute-done.1 = bf16[64,3584]{1,0:T(8,128)(2,1)S(1)} collective-permute-done((bf16[64,3584]{1,0:T(8,128)(2,1)}, bf16[64,3584]{1,0:T(8,128)(2,1)S(1)}, u32[]{:S(2)}, u32[]{:S(2)}) %collective-permute-start.1) | collective-permute-done | bytes 458784 | tf_op jit(solution)/shard_map/ppermute | solution.py:16
  346.0 31.9 %all_to_all.104 = bf16[64,2,3584]{2,1,0:T(2,128)(2,1)S(1)} all-to-all(bf16[64,2,3584]{2,1,0:T(2,128)(2,1)S(1)} %bitcast.286), channel_id=1, replica_groups=mesh['segment'=4,'expert'=64] {'expert'}, dimensions={0} | all-to-all | bytes 1835008 | tf_op jit(solution)/shard_map/all_to_all | solution.py:39
  379.2 2.3 fusion.44
  381.4 4.2 convolution_convert_fusion.5
  385.6 3.1 reshape.606
  388.7 6.1 all-to-all-start.9
  395.7 25.1 %all-to-all-done.9 = bf16[64,2,3584]{2,1,0:T(2,128)(2,1)S(1)} async-done(((bf16[64,2,3584]{2,1,0:T(2,128)(2,1)}), bf16[64,2,3584]{2,1,0:T(2,128)(2,1)S(1)}, u32[]{:S(2)}, u32[]{:S(2)}) %all-to-all-start.9) | async-done | bytes 917536 | tf_op jit(solution)/shard_map/all_to_all | solution.py:45
  420.8 1.5 convert_reduce_fusion.5
  426.3 31.6 %all_to_all.105 = bf16[64,2,3584]{2,1,0:T(2,128)(2,1)S(1)} all-to-all(bf16[64,2,3584]{2,1,0:T(2,128)(2,1)S(1)} %bitcast.287), channel_id=1, replica_groups=mesh['segment'=4,'expert'=64] {'expert'}, dimensions={0} | all-to-all | bytes 1835008 | tf_op jit(solution)/shard_map/all_to_all | solution.py:39
  459.2 2.3 fusion.19
  461.4 4.2 convolution_convert_fusion.4
  465.6 3.1 reshape.612
  468.7 5.7 all-to-all-start.11
  474.6 25.9 %all-to-all-done.11 = bf16[64,2,3584]{2,1,0:T(2,128)(2,1)S(1)} async-done(((bf16[64,2,3584]{2,1,0:T(2,128)(2,1)}), bf16[64,2,3584]{2,1,0:T(2,128)(2,1)S(1)}, u32[]{:S(2)}, u32[]{:S(2)}) %all-to-all-start.11) | async-done | bytes 917536 | tf_op jit(solution)/shard_map/all_to_all | solution.py:45
  502.4 1.8 fusion.243
  505.9 12.1 %collective-permute-done.2 = bf16[64,3584]{1,0:T(8,128)(2,1)S(1)} collective-permute-done((bf16[64,3584]{1,0:T(8,128)(2,1)}, bf16[64,3584]{1,0:T(8,128)(2,1)S(1)}, u32[]{:S(2)}, u32[]{:S(2)}) %collective-permute-start.2) | collective-permute-done | bytes 458784 | tf_op jit(solution)/shard_map/ppermute | solution.py:16
  519.2 32.1 %all_to_all.106 = bf16[64,2,3584]{2,1,0:T(2,128)(2,1)S(1)} all-to-all(bf16[64,2,3584]{2,1,0:T(2,128)(2,1)S(1)} %bitcast.288), channel_id=1, replica_groups=mesh['segment'=4,'expert'=64] {'expert'}, dimensions={0} | all-to-all | bytes 1835008 | tf_op jit(solution)/shard_map/all_to_all | solution.py:39
  552.5 2.3 fusion.42
  554.8 4.2 convolution_convert_fusion.3
  558.9 3.1 reshape.618
  562.0 5.7 all-to-all-start.13
  568.2 25.5 %all-to-all-done.13 = bf16[64,2,3584]{2,1,0:T(2,128)(2,1)S(1)} async-done(((bf16[64,2,3584]{2,1,0:T(2,128)(2,1)}), bf16[64,2,3584]{2,1,0:T(2,128)(2,1)S(1)}, u32[]{:S(2)}, u32[]{:S(2)}) %all-to-all-start.13) | async-done | bytes 917536 | tf_op jit(solution)/shard_map/all_to_all | solution.py:45
  593.8 1.5 convert_reduce_fusion.3
  599.3 31.6 %all_to_all.107 = bf16[64,2,3584]{2,1,0:T(2,128)(2,1)S(1)} all-to-all(bf16[64,2,3584]{2,1,0:T(2,128)(2,1)S(1)} %bitcast.289), channel_id=1, replica_groups=mesh['segment'=4,'expert'=64] {'expert'}, dimensions={0} | all-to-all | bytes 1835008 | tf_op jit(solution)/shard_map/all_to_all | solution.py:39
  632.1 2.3 fusion.17
  634.4 4.2 convolution_convert_fusion.2
  638.6 3.1 reshape.624
  641.6 5.9 all-to-all-start.15
  647.5 26.0 %all-to-all-done.15 = bf16[64,2,3584]{2,1,0:T(2,128)(2,1)S(1)} async-done(((bf16[64,2,3584]{2,1,0:T(2,128)(2,1)}), bf16[64,2,3584]{2,1,0:T(2,128)(2,1)S(1)}, u32[]{:S(2)}, u32[]{:S(2)}) %all-to-all-start.15) | async-done | bytes 917536 | tf_op jit(solution)/shard_map/all_to_all | solution.py:45
  677.3 12.3 %collective-permute-done.3 = bf16[64,3584]{1,0:T(8,128)(2,1)S(1)} collective-permute-done((bf16[64,3584]{1,0:T(8,128)(2,1)S(1)}, bf16[64,3584]{1,0:T(8,128)(2,1)S(1)}, u32[]{:S(2)}, u32[]{:S(2)}) %collective-permute-start.3) | collective-permute-done | bytes 458784 | tf_op jit(solution)/shard_map/ppermute | solution.py:16
  690.7 31.9 %all_to_all.108 = bf16[64,2,3584]{2,1,0:T(2,128)(2,1)S(1)} all-to-all(bf16[64,2,3584]{2,1,0:T(2,128)(2,1)S(1)} %bitcast.290), channel_id=1, replica_groups=mesh['segment'=4,'expert'=64] {'expert'}, dimensions={0} | all-to-all | bytes 1835008 | tf_op jit(solution)/shard_map/all_to_all | solution.py:39
  722.9 1.9 fusion.40
  724.8 3.2 convolution_convert_fusion.1
  729.4 5.7 all-to-all-start.17
  735.1 26.0 %all-to-all-done.17 = bf16[64,2,3584]{2,1,0:T(2,128)(2,1)S(1)} async-done(((bf16[64,2,3584]{2,1,0:T(2,128)(2,1)}), bf16[64,2,3584]{2,1,0:T(2,128)(2,1)S(1)}, u32[]{:S(2)}, u32[]{:S(2)}) %all-to-all-start.17) | async-done | bytes 917536 | tf_op jit(solution)/shard_map/all_to_all | solution.py:45
  764.2 31.8 %all_to_all.109 = bf16[64,2,3584]{2,1,0:T(2,128)(2,1)S(1)} all-to-all(bf16[64,2,3584]{2,1,0:T(2,128)(2,1)S(1)} %bitcast.291), channel_id=1, replica_groups=mesh['segment'=4,'expert'=64] {'expert'}, dimensions={0} | all-to-all | bytes 1835008 | tf_op jit(solution)/shard_map/all_to_all | solution.py:39
  796.4 1.9 fusion.15
  798.3 3.2 convolution_convert_fusion
  802.8 5.7 all-to-all-start.19
  809.5 25.1 %all-to-all-done.19 = bf16[64,2,3584]{2,1,0:T(2,128)(2,1)S(1)} async-done(((bf16[64,2,3584]{2,1,0:T(2,128)(2,1)}), bf16[64,2,3584]{2,1,0:T(2,128)(2,1)S(1)}, u32[]{:S(2)}, u32[]{:S(2)}) %all-to-all-start.19) | async-done | bytes 917536 | tf_op jit(solution)/shard_map/all_to_all | solution.py:45
  (198 shorter events, 66.6 us)
Async XLA Ops:
  49.0 7.6 copy-start.20
  50.3 31.8 %all-to-all-start.1 = ((bf16[64,2,3584]{2,1,0:T(2,128)(2,1)}), bf16[64,2,3584]{2,1,0:T(2,128)(2,1)S(1)}, u32[]{:S(2)}, u32[]{:S(2)}) async-start(bf16[64,2,3584]{2,1,0:T(2,128)(2,1)} %reshape.582), calls=%async_computation.1 | async-start | bytes 1835008 | tf_op jit(solution)/shard_map/all_to_all | solution.py:45
  83.0 1.2 copy-start
  123.8 31.9 %all-to-all-start.3 = ((bf16[64,2,3584]{2,1,0:T(2,128)(2,1)}), bf16[64,2,3584]{2,1,0:T(2,128)(2,1)S(1)}, u32[]{:S(2)}, u32[]{:S(2)}) async-start(bf16[64,2,3584]{2,1,0:T(2,128)(2,1)} %reshape.588), calls=%async_computation.3 | async-start | bytes 1835008 | tf_op jit(solution)/shard_map/all_to_all | solution.py:45
  158.7 13.8 %collective-permute-start = (bf16[64,3584]{1,0:T(8,128)(2,1)}, bf16[64,3584]{1,0:T(8,128)(2,1)S(1)}, u32[]{:S(2)}, u32[]{:S(2)}) collective-permute-start(bf16[64,3584]{1,0:T(8,128)(2,1)} %get-tuple-element.71), channel_id=1, source_target_pairs={{0,64},{64,128},{128,192},{1,65},{65,129},{129,193},{2,66},{66,130... | collective-permute-start | bytes 1376264 | tf_op jit(solution)/shard_map/ppermute | solution.py:16
  206.8 2.3 copy-start.7
  216.3 31.8 %all-to-all-start.5 = ((bf16[64,2,3584]{2,1,0:T(2,128)(2,1)}), bf16[64,2,3584]{2,1,0:T(2,128)(2,1)S(1)}, u32[]{:S(2)}, u32[]{:S(2)}) async-start(bf16[64,2,3584]{2,1,0:T(2,128)(2,1)} %reshape.594), calls=%async_computation.5 | async-start | bytes 1835008 | tf_op jit(solution)/shard_map/all_to_all | solution.py:45
  251.6 1.2 copy-start.21
  252.0 0.8 copy-start.3
  286.6 2.3 copy-start.8
  293.1 8.8 %copy-start.18 = (s32[64]{0:T(128)S(1)}, s32[64]{0:T(128)}, u32[]{:S(2)}) copy-start(s32[64]{0:T(128)} %get-tuple-element.59) | copy-start | bytes 772
  296.2 31.8 %all-to-all-start.7 = ((bf16[64,2,3584]{2,1,0:T(2,128)(2,1)}), bf16[64,2,3584]{2,1,0:T(2,128)(2,1)S(1)}, u32[]{:S(2)}, u32[]{:S(2)}) async-start(bf16[64,2,3584]{2,1,0:T(2,128)(2,1)} %reshape.600), calls=%async_computation.7 | async-start | bytes 1835008 | tf_op jit(solution)/shard_map/all_to_all | solution.py:45
  328.9 1.0 copy-start.4
  328.9 1.0 copy-start.17
  331.1 13.8 %collective-permute-start.1 = (bf16[64,3584]{1,0:T(8,128)(2,1)}, bf16[64,3584]{1,0:T(8,128)(2,1)S(1)}, u32[]{:S(2)}, u32[]{:S(2)}) collective-permute-start(bf16[64,3584]{1,0:T(8,128)(2,1)} %get-tuple-element.55), channel_id=1, source_target_pairs={{0,64},{64,128},{128,192},{1,65},{65,129},{129,193},{2,66},{66,130... | collective-permute-start | bytes 1376264 | tf_op jit(solution)/shard_map/ppermute | solution.py:16
  379.1 2.3 copy-start.9
  388.7 32.2 %all-to-all-start.9 = ((bf16[64,2,3584]{2,1,0:T(2,128)(2,1)}), bf16[64,2,3584]{2,1,0:T(2,128)(2,1)S(1)}, u32[]{:S(2)}, u32[]{:S(2)}) async-start(bf16[64,2,3584]{2,1,0:T(2,128)(2,1)} %reshape.606), calls=%async_computation.9 | async-start | bytes 1835008 | tf_op jit(solution)/shard_map/all_to_all | solution.py:45
  423.4 0.9 copy-start.16
  424.7 0.8 copy-start.1
  459.2 2.3 copy-start.10
  465.6 8.9 %copy-start.19 = (s32[64]{0:T(128)S(1)}, s32[64]{0:T(128)}, u32[]{:S(2)}) copy-start(s32[64]{0:T(128)} %get-tuple-element.43) | copy-start | bytes 772
  468.7 31.8 %all-to-all-start.11 = ((bf16[64,2,3584]{2,1,0:T(2,128)(2,1)}), bf16[64,2,3584]{2,1,0:T(2,128)(2,1)S(1)}, u32[]{:S(2)}, u32[]{:S(2)}) async-start(bf16[64,2,3584]{2,1,0:T(2,128)(2,1)} %reshape.612), calls=%async_computation.11 | async-start | bytes 1835008 | tf_op jit(solution)/shard_map/all_to_all | solution.py:45
  501.4 1.0 copy-start.2
  504.2 13.8 %collective-permute-start.2 = (bf16[64,3584]{1,0:T(8,128)(2,1)}, bf16[64,3584]{1,0:T(8,128)(2,1)S(1)}, u32[]{:S(2)}, u32[]{:S(2)}) collective-permute-start(bf16[64,3584]{1,0:T(8,128)(2,1)} %get-tuple-element.39), channel_id=1, source_target_pairs={{0,64},{64,128},{128,192},{1,65},{65,129},{129,193},{2,66},{66,130... | collective-permute-start | bytes 1376264 | tf_op jit(solution)/shard_map/ppermute | solution.py:16
  552.5 2.3 copy-start.11
  562.0 31.8 %all-to-all-start.13 = ((bf16[64,2,3584]{2,1,0:T(2,128)(2,1)}), bf16[64,2,3584]{2,1,0:T(2,128)(2,1)S(1)}, u32[]{:S(2)}, u32[]{:S(2)}) async-start(bf16[64,2,3584]{2,1,0:T(2,128)(2,1)} %reshape.618), calls=%async_computation.13 | async-start | bytes 1835008 | tf_op jit(solution)/shard_map/all_to_all | solution.py:45
  596.3 0.9 copy-start.14
  597.7 0.8 copy-start.5
  632.1 2.3 copy-start.12
  641.6 32.0 %all-to-all-start.15 = ((bf16[64,2,3584]{2,1,0:T(2,128)(2,1)}), bf16[64,2,3584]{2,1,0:T(2,128)(2,1)S(1)}, u32[]{:S(2)}, u32[]{:S(2)}) async-start(bf16[64,2,3584]{2,1,0:T(2,128)(2,1)} %reshape.624), calls=%async_computation.15 | async-start | bytes 1835008 | tf_op jit(solution)/shard_map/all_to_all | solution.py:45
  674.5 1.0 copy-start.6
  674.5 1.0 copy-start.15
  676.0 13.6 %collective-permute-start.3 = (bf16[64,3584]{1,0:T(8,128)(2,1)S(1)}, bf16[64,3584]{1,0:T(8,128)(2,1)S(1)}, u32[]{:S(2)}, u32[]{:S(2)}) collective-permute-start(bf16[64,3584]{1,0:T(8,128)(2,1)S(1)} %get-tuple-element.23), channel_id=1, source_target_pairs={{0,64},{64,128},{128,192},{1,65},{65,129},{129,193},{2,66},{66,130... | collective-permute-start | bytes 1376264 | tf_op jit(solution)/shard_map/ppermute | solution.py:16
  729.4 31.8 %all-to-all-start.17 = ((bf16[64,2,3584]{2,1,0:T(2,128)(2,1)}), bf16[64,2,3584]{2,1,0:T(2,128)(2,1)S(1)}, u32[]{:S(2)}, u32[]{:S(2)}) async-start(bf16[64,2,3584]{2,1,0:T(2,128)(2,1)} %reshape.631), calls=%async_computation.17 | async-start | bytes 1835008 | tf_op jit(solution)/shard_map/all_to_all | solution.py:45
  802.8 31.8 %all-to-all-start.19 = ((bf16[64,2,3584]{2,1,0:T(2,128)(2,1)}), bf16[64,2,3584]{2,1,0:T(2,128)(2,1)S(1)}, u32[]{:S(2)}, u32[]{:S(2)}) async-start(bf16[64,2,3584]{2,1,0:T(2,128)(2,1)} %reshape.637), calls=%async_computation.19 | async-start | bytes 1835008 | tf_op jit(solution)/shard_map/all_to_all | solution.py:45
  835.5 0.9 copy-start.13
where the time goes:
time: 848 us; the launch traced here: 838 us
  blocking collectives  324 us (38%)
  waiting for transfers between devices  304 us (36%)
  matrix products  63 us (7%)
  starting transfers between devices  62.7 us (7%)
  local copies, waits for them, and re-layouts  57.7 us (7%)
  other arithmetic  24.5 us (3%)
    all_to_all x10, blocking collectives, moe_layer(): lax.all_to_all(spread, 'expert', split_axis=0, concat_axis=0, tiled=True)  324 us
    all_to_all x10, waiting for transfers between devices, moe_layer(): lax.all_to_all(partial_value.reshape(received.shape), 'expert', split_axi...  256 us
    all_to_all x10, starting transfers between devices, moe_layer(): lax.all_to_all(partial_value.reshape(received.shape), 'expert', split_axi...  57.6 us
    ppermute x4, waiting for transfers between devices, from_behind(): lax.ppermute(value, axis, [(source, source + steps) for source in range(l...  47.8 us
    dot_general x10, matrix products, moe_layer(): jnp.dot(hidden, down_w, preferred_element_type=jnp.float32)  37.9 us
    reshape x10, local copies, waits for them, and re-layouts, moe_layer(): partial_value.reshape(received.shape)  23.5 us
    dot_general x10, matrix products, moe_layer(): gate_pre = jnp.dot(flattened, gate_w, preferred_element_type=jnp.float32)  21.2 us
  transfers between devices with their start and end apart: 14, of which 14 were waited for; matrix products, arithmetic and copies ran while one was open for 1% of the time, Pallas kernels for 0%

commit v1 on v0

v1 whole, which is shorter than its diff:
```python
import functools

import jax
import jax.numpy as jnp
from jax import lax
from jax.experimental import pallas as pl
from jax.experimental.pallas import tpu as pltpu
from jax.sharding import PartitionSpec as P

MESH = pl.DeviceIdType.MESH
LMAX = 2
MB = 2
TOK = 64
Z = 8
Y = 4
PIECE = 512
FAR_FIRST = (4, 3, 5, 2, 6, 1, 7, 0)


def iota(shape, dim):
    return lax.broadcasted_iota(jnp.int32, shape, dim)


def ones_where(condition):
    return jnp.where(condition, 1.0, 0.0).astype(jnp.bfloat16)


def dot(a, b):
    return jnp.dot(a, b, preferred_element_type=jnp.float32)


def kernel(
    starts,
    steps,
    tokens_ref,
    gain_ref,
    gate_hbm,
    up_hbm,
    down_hbm,
    ids_ref,
    ids_col_ref,
    scale_ref,
    depth_ref,
    out_ref,
    gate_w,
    up_w,
    down_w,
    state,
    ids_next,
    pack_m,
    unpack_m,
    perm,
    perm_t,
    sent,
    landed,
    gathered,
    part,
    sibling_part,
    pair,
    reduced,
    back,
    returned,
    weight_sem,
    state_sem,
    ids_sem,
    sent_sem,
    landed_sem,
    gather_send_sem,
    gather_sem,
    sib_sem,
    reduce_send_sem,
    reduce_sem,
    back_sem,
    returned_sem,
):
    x = lax.axis_index("segment")
    me = lax.axis_index("expert")
    segments = lax.axis_size("segment")
    z = me // (Y * 2)
    y = (me // 2) % Y
    c = me % 2
    width = tokens_ref.shape[2]
    pieces = width // PIECE
    group = Y * 16

    def at(xx, zz, yy, cc):
        return (xx, zz * (Y * 2) + yy * 2 + cc)

    loads = []
    for layer in range(LMAX):
        for i, (src, dst) in enumerate(((gate_hbm, gate_w), (up_hbm, up_w), (down_hbm, down_w))):
            load = pltpu.make_async_copy(src.at[0, layer], dst.at[layer], weight_sem.at[layer, i])
            load.start()
            loads.append(load)

    barrier = pltpu.get_barrier_semaphore()

    def greet(device):
        pl.semaphore_signal(barrier, inc=1, device_id=device, device_id_type=MESH)

    for d in range(1, Z):
        greet(at(x, (z + d) % Z, y, c))
    for d in range(1, Y):
        greet(at(x, z, (y + d) % Y, c))
    greet(at(x, z, y, 1 - c))

    @pl.when(x > 0)
    def _():
        for d in range(Z):
            greet(at(x - 1, (z + d) % Z, y, c))

    @pl.when(x < segments - 1)
    def _():
        for d in range(Z):
            greet(at(x + 1, (z + d) % Z, y, c))

    @pl.when((x == 0) | (x == segments - 1))
    def _():
        pl.semaphore_wait(barrier, 11 + Z)

    @pl.when((x > 0) & (x < segments - 1))
    def _():
        pl.semaphore_wait(barrier, 11 + 2 * Z)

    ids_copy = pltpu.make_async_remote_copy(
        src_ref=ids_ref,
        dst_ref=ids_next,
        send_sem=ids_sem.at[0],
        recv_sem=ids_sem.at[1],
        device_id=at(jnp.maximum(x - 1, 0), z, y, c),
        device_id_type=MESH,
    )

    @pl.when(x > 0)
    def _():
        ids_copy.start()

    lanes = pieces * TOK
    row = iota((128, lanes), 0)
    col = iota((128, lanes), 1)
    row_e, row_j, row_k = row // 16, (row // 2) % 8, row % 2
    earlier = ones_where(iota((TOK, lanes), 0) <= iota((TOK, lanes), 1) % TOK)
    same_j = row_j == col // TOK

    def packing(ids_row):
        hit = ones_where(jnp.broadcast_to(ids_row, (128, lanes)) == row_e)
        rank = dot(hit[:, :TOK], earlier)
        good = (hit > 0) & (rank == (row_k + 1).astype(jnp.float32)) & same_j
        return ones_where(good)

    slot = iota((TOK, 128), 1)
    slot_e, slot_j, slot_k = slot // 16, (slot // 2) % 8, slot % 2
    earlier_t = ones_where(iota((TOK, TOK), 1) <= iota((TOK, TOK), 0))

    def dispatch_copy(m, zz, to):
        return pltpu.make_async_remote_copy(
            src_ref=sent.at[m, zz],
            dst_ref=landed.at[m, z],
            send_sem=sent_sem.at[m, zz],
            recv_sem=landed_sem.at[m, z],
            device_id=at(to, zz, y, c),
            device_id_type=MESH,
        )

    def own_copy(m):
        return pltpu.make_async_copy(sent.at[m, z], landed.at[m, z], landed_sem.at[m, z])

    def dispatch(which, m, to):
        sent[m] = (
            dot(pack_m[which, m], state[m])
            .astype(jnp.bfloat16)
            .reshape(Z, 16, PIECE)
        )
        for d in FAR_FIRST[:-1]:
            dispatch_copy(m, (z + d) % Z, to).start()

        @pl.when(to == x)
        def _():
            own_copy(m).start()

        @pl.when(to != x)
        def _():
            dispatch_copy(m, z, to).start()

    def dispatch_sent(m, to):
        for d in FAR_FIRST[:-1]:
            dispatch_copy(m, (z + d) % Z, to).wait_send()

        @pl.when(to != x)
        def _():
            dispatch_copy(m, z, to).wait_send()

    @pl.when(x == 0)
    def _():
        for m in range(MB):
            for j in range(pieces):
                state[m, j * TOK : (j + 1) * TOK] = tokens_ref[m, :, j * PIECE : (j + 1) * PIECE]
            pack_m[0, m] = packing(ids_ref[m : m + 1, :])
            dispatch(0, m, 0)

    for m in range(MB):
        pack_m[1, m] = packing(ids_ref[MB + m : MB + m + 1, :])

    p_row, p_col = iota((128, 128), 0), iota((128, 128), 1)
    perm[...] = ones_where(
        (p_col == ((p_row // 2) % 8) * 16 + (p_row // 16) * 2 + p_row % 2)
        & ((p_row // 2) % 8 < pieces)
    )
    perm_t[...] = ones_where(
        (p_row == ((p_col // 2) % 8) * 16 + (p_col // 16) * 2 + p_col % 2)
        & ((p_col // 2) % 8 < pieces)
    )
    for layer in range(LMAX):
        for m in range(MB):
            ids_col = ids_col_ref[:, layer * MB + m : layer * MB + m + 1]
            hit = ones_where(jnp.broadcast_to(ids_col, (TOK, 128)) == slot_e)
            rank = dot(earlier_t, hit)
            good = (hit > 0) & (rank == (slot_k + 1).astype(jnp.float32))
            for j in range(pieces):
                unpack_m[layer, m, j * TOK : (j + 1) * TOK] = ones_where(good & (slot_j == j))

    @pl.when(x < segments - 1)
    def _():
        ids_copy.wait_recv()
        for m in range(MB):
            pack_m[2, m] = packing(ids_next[m : m + 1, :])

    @pl.when(x > 0)
    def _():
        ids_copy.wait_send()

    for load in loads:
        load.wait()

    def section_of(k):
        total = jnp.int32(0)
        for start in starts[1:]:
            total = total + jnp.where(k >= start, 1, 0)
        return total

    def layer_of(k):
        total = k
        for before, start in zip(starts[:-1], starts[1:]):
            total = total - jnp.where(k >= start, start - before, 0)
        return total

    def state_copy(m):
        return pltpu.make_async_remote_copy(
            src_ref=state.at[m],
            dst_ref=state.at[m],
            send_sem=state_sem.at[0, m],
            recv_sem=state_sem.at[1, m],
            device_id=at(jnp.minimum(x + 1, segments - 1), z, y, c),
            device_id_type=MESH,
        )

    mine = c * Y + y

    def gather_copies(m):
        copies = []
        for d in (2, 1, 3):
            copies.append(
                pltpu.make_async_remote_copy(
                    src_ref=gathered.at[m, mine],
                    dst_ref=gathered.at[m, mine],
                    send_sem=gather_send_sem.at[m, d],
                    recv_sem=gather_sem.at[m, mine],
                    device_id=at(x, z, (y + d) % Y, c),
                    device_id_type=MESH,
                )
            )
        return copies

    def forward(m, yy, i):
        block = c * Y + yy
        return pltpu.make_async_remote_copy(
            src_ref=gathered.at[m, block],
            dst_ref=gathered.at[m, block],
            send_sem=gather_send_sem.at[m, 4 + i],
            recv_sem=gather_sem.at[m, block],
            device_id=at(x, z, y, 1 - c),
            device_id_type=MESH,
        )

    def arrived(m, block):
        pltpu.make_async_copy(
            gathered.at[m, block], gathered.at[m, block], gather_sem.at[m, block]
        ).wait()

    def relay(m, layer):
        for d in range(Z):
            zz = (z + d) % Z
            pltpu.make_async_copy(landed.at[m, zz], landed.at[m, zz], landed_sem.at[m, zz]).wait()
        rows = dot(perm_t[...], landed[m].reshape(128, PIECE))
        square = jnp.zeros((16, 1), jnp.float32)
        for j in range(pieces):
            piece = rows[16 * j : 16 * j + 16]
            square = square + jnp.sum(piece * piece, axis=1, keepdims=True)
        ratio = lax.rsqrt(square / width + 1e-06)
        gain = gain_ref[0, pl.ds(layer, 1), :]
        for j in range(pieces):
            span = slice(j * PIECE, (j + 1) * PIECE)
            gathered[m, mine, :, span] = (
                rows[16 * j : 16 * j + 16] * ratio * gain[:, span]
            ).astype(jnp.bfloat16)
        for copy in gather_copies(m):
            copy.start()
        forward(m, y, 0).start()

    def pass_on(m):
        for i, d in enumerate((1, 3, 2)):
            yy = (y + d) % Y
            arrived(m, c * Y + yy)
            forward(m, yy, i + 1).start()

    def sibling_copy(m):
        return pltpu.make_async_remote_copy(
            src_ref=part.at[m, 1 - c],
            dst_ref=sibling_part.at[m],
            send_sem=sib_sem.at[0, m],
            recv_sem=sib_sem.at[1, m],
            device_id=at(x, z, y, 1 - c),
            device_id_type=MESH,
        )

    def experts(m, layer):
        for yy in range(Y):
            arrived(m, (1 - c) * Y + yy)
        rows = gathered[m].reshape(128, width)
        gate = dot(rows, gate_w[layer])
        up = dot(rows, up_w[layer])
        hidden = (gate * lax.logistic(gate) * up).astype(jnp.bfloat16)
        for j in range(pieces):
            span = slice(j * PIECE, (j + 1) * PIECE)
            part[m, :, :, span] = (
                dot(hidden, down_w[layer, :, span]).astype(jnp.bfloat16).reshape(2, group, PIECE)
            )
        sibling_copy(m).start()

    def reduce_copy(m, d):
        return pltpu.make_async_remote_copy(
            src_ref=pair.at[m, (y + d) % Y],
            dst_ref=reduced.at[m, y],
            send_sem=reduce_send_sem.at[m, d],
            recv_sem=reduce_sem.at[m, y],
            device_id=at(x, z, (y + d) % Y, c),
            device_id_type=MESH,
        )

    def chip_sum(m):
        for copy in gather_copies(m):
            copy.wait_send()
        for i, d in enumerate((0, 1, 3, 2)):
            forward(m, (y + d) % Y, i).wait_send()
        sibling_copy(m).wait_recv()
        for d in (2, 1, 3, 0):
            yy = (y + d) % Y
            start = pl.multiple_of(yy * 16, 16)
            pair[m, yy] = (
                part[m, c, pl.ds(start, 16), :].astype(jnp.float32)
                + sibling_part[m, pl.ds(start, 16), :].astype(jnp.float32)
            ).astype(jnp.bfloat16)
            if d > 0:
                reduce_copy(m, d).start()

    def back_copy(m, zz):
        return pltpu.make_async_remote_copy(
            src_ref=back.at[m, zz],
            dst_ref=returned.at[m, z],
            send_sem=back_sem.at[m, zz],
            recv_sem=returned_sem.at[m, z],
            device_id=at(x, zz, y, c),
            device_id_type=MESH,
        )

    def own_back(m):
        return pltpu.make_async_copy(back.at[m, z], returned.at[m, z], returned_sem.at[m, z])

    def plane_sum(m):
        for d in (1, 3, 2):
            yy = (y + d) % Y
            pltpu.make_async_copy(
                reduced.at[m, yy], reduced.at[m, yy], reduce_sem.at[m, yy]
            ).wait()
        total = []
        for j in range(pieces):
            span = slice(j * PIECE, (j + 1) * PIECE)
            value = pair[m, y, :, span].astype(jnp.float32)
            for d in range(1, Y):
                value = value + reduced[m, (y + d) % Y, :, span].astype(jnp.float32)
            total.append(value.astype(jnp.bfloat16))
        stacked = jnp.concatenate(total, axis=0)
        back[m] = (
            dot(perm[:, : 16 * pieces], stacked).astype(jnp.bfloat16).reshape(Z, 16, PIECE)
        )
        for d in FAR_FIRST[:-1]:
            back_copy(m, (z + d) % Z).start()
        own_back(m).start()

    def combine(m, layer):
        for d in range(Z):
            zz = (z + d) % Z
            pltpu.make_async_copy(
                returned.at[m, zz], returned.at[m, zz], returned_sem.at[m, zz]
            ).wait()
        values = returned[m].reshape(128, PIECE)
        active = layer < depth_ref[0]
        column = jnp.where(layer == 0, scale_ref[:, m : m + 1], scale_ref[:, MB + m : MB + m + 1])
        for j in range(pieces):
            span = slice(j * TOK, (j + 1) * TOK)
            picked = dot(unpack_m[layer, m, span], values)
            before = state[m, span].astype(jnp.float32)
            after = before + column * picked
            state[m, span] = jnp.where(active, after, before).astype(jnp.bfloat16)

    def finish(m):
        sibling_copy(m).wait_send()
        for d in range(1, Y):
            reduce_copy(m, d).wait_send()
        for d in FAR_FIRST[:-1]:
            back_copy(m, (z + d) % Z).wait_send()

    @pl.when(x == 0)
    def _():
        for m in range(MB):
            dispatch_sent(m, 0)

    def step(k, carry):
        section = section_of(k)
        layer = layer_of(k)
        section_after = section_of(k + 1)
        last = section_after != section

        @pl.when(x == section)
        def _():
            relay(0, layer)
            relay(1, layer)
            pass_on(0)
            experts(0, layer)
            pass_on(1)
            chip_sum(0)
            experts(1, layer)
            chip_sum(1)
            plane_sum(0)
            plane_sum(1)
            for m in range(MB):

                @pl.when((layer == 0) & (section > 0))
                def _():
                    pltpu.make_async_copy(state.at[m], state.at[m], state_sem.at[1, m]).wait()

                combine(m, layer)

                @pl.when(k + 1 < steps)
                def _():
                    dispatch(jnp.where(last, 2, 1), m, section_after)

                @pl.when((k + 1 < steps) & last)
                def _():
                    state_copy(m).start()

            for m in range(MB):
                finish(m)

                @pl.when(k + 1 < steps)
                def _():
                    dispatch_sent(m, section_after)

        return carry

    lax.fori_loop(0, steps, step, 0)

    for m in range(MB):
        for j in range(pieces):
            out_ref[0, m, :, j * PIECE : (j + 1) * PIECE] = state[m, j * TOK : (j + 1) * TOK]

    @pl.when(x < segments - 1)
    def _():
        for m in range(MB):
            state_copy(m).wait_send()


def run(depths_static, collective, args):
    tokens, gain, gate, up, down, ids, ids_col, scale, depth = args
    starts, total = [], 0
    for d in depths_static:
        starts.append(total)
        total += d
    width = tokens.shape[2]
    hidden = gate.shape[3]
    lanes = width // PIECE * TOK
    vmem = pl.BlockSpec(memory_space=pltpu.VMEM)
    hbm = pl.BlockSpec(memory_space=pl.ANY)
    bf = jnp.bfloat16
    dma = pltpu.SemaphoreType.DMA
    return pl.pallas_call(
        functools.partial(kernel, tuple(starts), total),
        out_shape=jax.ShapeDtypeStruct((1, MB, TOK, width), bf),
        in_specs=[vmem, vmem, hbm, hbm, hbm, vmem, vmem, vmem, pl.BlockSpec(memory_space=pltpu.SMEM)],
        out_specs=vmem,
        scratch_shapes=[
            pltpu.VMEM((LMAX, width, hidden), bf),
            pltpu.VMEM((LMAX, width, hidden), bf),
            pltpu.VMEM((LMAX, hidden, width), bf),
            pltpu.VMEM((MB, lanes, PIECE), bf),
            pltpu.VMEM((8, lanes), jnp.int32),
            pltpu.VMEM((3, MB, 128, lanes), bf),
            pltpu.VMEM((LMAX, MB, lanes, 128), bf),
            pltpu.VMEM((128, 128), bf),
            pltpu.VMEM((128, 128), bf),
            pltpu.VMEM((MB, Z, 16, PIECE), bf),
            pltpu.VMEM((MB, Z, 16, PIECE), bf),
            pltpu.VMEM((MB, 8, 16, width), bf),
            pltpu.VMEM((MB, 2, Y * 16, width), bf),
            pltpu.VMEM((MB, Y * 16, width), bf),
            pltpu.VMEM((MB, Y, 16, width), bf),
            pltpu.VMEM((MB, Y, 16, width), bf),
            pltpu.VMEM((MB, Z, 16, PIECE), bf),
            pltpu.VMEM((MB, Z, 16, PIECE), bf),
            dma((LMAX, 3)),
            dma((2, MB)),
            dma((2,)),
            dma((MB, Z)),
            dma((MB, Z)),
            dma((MB, 8)),
            dma((MB, 8)),
            dma((2, MB)),
            dma((MB, Y)),
            dma((MB, Y)),
            dma((MB, Z)),
            dma((MB, Z)),
        ],
        compiler_params=pltpu.CompilerParams(
            collective_id=collective, has_side_effects=True, vmem_limit_bytes=48 * 2**20
        ),
        name="relay_layers",
    )(tokens, gain, gate, up, down, ids, ids_col, scale, depth)


def local(tokens, norm_gain, gate_weight, up_weight, down_weight, expert_ids, gate_scale, depths):
    pieces = tokens.shape[2] // PIECE
    ids = expert_ids.reshape(LMAX * MB, TOK)
    ids_rows = jnp.pad(jnp.tile(ids, (1, pieces)), ((0, 8 - LMAX * MB), (0, 0)))
    ids_col = ids.T
    scale = gate_scale.reshape(LMAX * MB, TOK).T
    args = (
        tokens,
        norm_gain,
        gate_weight,
        up_weight,
        down_weight,
        ids_rows,
        ids_col,
        scale,
        depths,
    )
    return run((2, 2, 2, 2), 0, args)


def solution(mesh):
    return jax.shard_map(
        local,
        mesh=mesh,
        in_specs=(
            P(None, "expert", None),
            P("segment", None, None),
            P("segment", None, None, "expert"),
            P("segment", None, None, "expert"),
            P("segment", None, "expert", None),
            P("segment", None, None, "expert"),
            P("segment", None, None, "expert"),
            P("segment"),
        ),
        out_specs=P("segment", None, "expert", None),
        check_vma=False,
    )
```

time: 848 us -> 293 us (0.35); the launches traced: 838 us -> 293 us
  blocking collectives: 324 us -> 0 us
  waiting for transfers between devices: 304 us -> 0 us
  Pallas kernels: 0 us -> 285 us
  matrix products: 63 us -> 0 us
  starting transfers between devices: 62.7 us -> 0 us
  local copies, waits for them, and re-layouts: 57.7 us -> 7.2 us
  other arithmetic: 24.5 us -> 0 us
    all_to_all x10 -> x0, blocking collectives: 324 us -> none  [moe_layer(): lax.all_to_all(spread, 'expert', split_axis=0, concat_axis=0, tiled=True)]
    pallas_call x0 -> x1, Pallas kernels: none -> 285 us  [run(): pl.pallas_call(functools.partial(kernel, tuple(starts), total), out_shape...]
    all_to_all x10 -> x0, waiting for transfers between devices: 256 us -> none  [moe_layer(): lax.all_to_all(partial_value.reshape(received.shape), 'expert', split_axi...]
    dot_general x30 -> x0, matrix products: 63 us -> none  [the longest x10 37.9 us: moe_layer(): jnp.dot(hidden, down_w, preferred_element_type=jnp.float32)]
    all_to_all x10 -> x0, starting transfers between devices: 57.6 us -> none  [moe_layer(): lax.all_to_all(partial_value.reshape(received.shape), 'expert', split_axi...]
    ppermute x4 -> x0, waiting for transfers between devices: 47.8 us -> none  [from_behind(): lax.ppermute(value, axis, [(source, source + steps) for source in range(l...]
    reshape x30 -> x1, local copies, waits for them, and re-layouts: 36.9 us -> 0.77 us  [local(): scale = gate_scale.reshape(LMAX * MB, TOK).T]
    reduce_sum x28 -> x0, other arithmetic: 15.7 us -> none  [the longest x10 9.85 us: moe_layer(): jnp.sum(returned.astype(jnp.float32).reshape(window_experts, GROUP, capac...]
  transfers between devices with their start and end apart: 14 -> 0, of which waited for: 14 -> 0; matrix products, arithmetic and copies ran while one was open for 1% -> 0% of each run, Pallas kernels for 0% -> 0%
where the time goes in v1:
time: 293 us
  Pallas kernels  285 us (97%)
  local copies, waits for them, and re-layouts  7.2 us (2%)
    pallas_call x1, Pallas kernels, run(): pl.pallas_call(functools.partial(kernel, tuple(starts), total), out_shape...  285 us

profile of v1, /device:TPU:6, one launch (start us, length us, event | category | flops | bytes accessed | tf_op | source)
XLA Modules:
  0.0 292.9 jit_solution(706051300929867846)
XLA Ops:
  0.7 0.7 tile.11
  1.3 0.1 tile.12
  1.4 0.8 copy.12
  2.2 0.8 copy.13
  3.0 0.0 copy-start
  3.0 2.0 copy-done
  5.0 0.0 copy-start.1
  5.0 1.2 copy-done.1
  6.2 0.0 copy-start.2
  6.2 0.7 copy-done.2
  6.9 285.0 %relay_layers.1 = bf16[1,2,64,3584]{3,2,1,0:T(8,128)(2,1)S(1)} custom-call(bf16[2,64,3584]{2,1,0:T(8,128)(2,1)S(1)} %copy-done.1, f32[1,2,3584]{2,1,0:T(2,128)S(1)} %copy-done.2, bf16[1,2,3584,256]{3,2,1,0:T(8,128)(2,1)S(1)} %copy-done, bf16[1,2,3584,256]{3,2,1,0:T(8,128)(2,1)} %up_hbm.1, bf16[1,2,256,3584]{3,2,1,0:T(8,128)(2,1)} %down_hbm.1, ...), custom_call_target="tpu_custom_call" | custom-call | tf_op jit(solution)/shard_map/relay_layers/pallas_call | solution.py:496
  292.0 0.9 copy.16
  (1 shorter events, 0.0 us)
Async XLA Ops:
  3.0 2.0 copy-start
  5.0 1.2 copy-start.1
  6.2 0.7 copy-start.2

commit v2 on v1

v2 whole, which is shorter than its diff:
```python
import functools

import jax
import jax.numpy as jnp
from jax import lax
from jax.experimental import pallas as pl
from jax.experimental.pallas import tpu as pltpu
from jax.sharding import PartitionSpec as P

MESH = pl.DeviceIdType.MESH
LMAX = 2
MB = 2
TOK = 64
Z = 8
Y = 4
PIECE = 512


def iota(shape, dim):
    return lax.broadcasted_iota(jnp.int32, shape, dim)


def ones_where(condition):
    return jnp.where(condition, 1.0, 0.0).astype(jnp.bfloat16)


def dot(a, b):
    return jnp.dot(a, b, preferred_element_type=jnp.float32)


def kernel(
    starts,
    steps,
    tokens_hbm,
    gain_ref,
    gate_hbm,
    up_hbm,
    down_hbm,
    ids_ref,
    scale_ref,
    out_ref,
    gate_w,
    up_w,
    down_w,
    state,
    ids_own,
    ids_next,
    scale_cols,
    mask,
    pack_m,
    unpack_m,
    perm,
    perm_t,
    both,
    sent,
    landed,
    gathered,
    part,
    sibling_part,
    pair,
    reduced,
    back,
    returned,
    token_sem,
    weight_sem,
    state_sem,
    ids_sem,
    sent_sem,
    landed_sem,
    gather_send_sem,
    gather_sem,
    sib_sem,
    reduce_send_sem,
    reduce_sem,
    back_sem,
    returned_sem,
):
    x = lax.axis_index("segment")
    me = lax.axis_index("expert")
    segments = lax.axis_size("segment")
    z = me // (Y * 2)
    y = (me // 2) % Y
    c = me % 2
    width = gathered.shape[3]
    pieces = width // PIECE
    group = Y * 16

    def at(xx, zz, yy, cc):
        return (xx, zz * (Y * 2) + yy * 2 + cc)

    def each(count, body):
        lax.fori_loop(0, count, lambda i, carry: (body(i), carry)[1], 0)

    def far(i):
        return 4 + ((i + 1) // 2) * (1 - 2 * (i % 2))

    def weight_load(layer, i):
        src, dst = ((gate_hbm, gate_w), (up_hbm, up_w), (down_hbm, down_w))[i]
        return pltpu.make_async_copy(src.at[0, layer], dst.at[layer], weight_sem.at[layer, i])

    def token_load(m, j):
        return pltpu.make_async_copy(
            tokens_hbm.at[m, :, pl.ds(j * PIECE, PIECE)],
            state.at[m, pl.ds(j * TOK, TOK)],
            token_sem.at[m, j],
        )

    barrier = pltpu.get_barrier_semaphore()

    def greet(device):
        pl.semaphore_signal(barrier, inc=1, device_id=device, device_id_type=MESH)

    each(Z - 1, lambda i: greet(at(x, (z + i + 1) % Z, y, c)))
    each(Y - 1, lambda i: greet(at(x, z, (y + i + 1) % Y, c)))
    greet(at(x, z, y, 1 - c))

    @pl.when(x > 0)
    def _():
        each(Z, lambda i: greet(at(x - 1, (z + i) % Z, y, c)))

    @pl.when(x < segments - 1)
    def _():
        each(Z, lambda i: greet(at(x + 1, (z + i) % Z, y, c)))

    @pl.when(x == 0)
    def _():
        each(MB * pieces, lambda i: token_load(i // pieces, i % pieces).start())

    for layer in range(LMAX):
        for i in range(3):
            weight_load(layer, i).start()

    lanes = pieces * TOK
    spread = ones_where(iota((TOK, lanes), 0) == iota((TOK, lanes), 1) % TOK)
    row_slot = iota((128, 16), 0)
    to_row = ones_where((row_slot // 16) * 2 + row_slot % 2 == iota((128, 16), 1))
    mask[...] = ones_where((iota((128, lanes), 0) // 2) % 8 == iota((128, lanes), 1) // TOK)
    ids_own[...] = jnp.zeros_like(ids_own)
    ids_own[0 : LMAX * MB, :TOK] = ids_ref[...].astype(jnp.float32)

    def slots(rows_ref, index):
        slot = iota((16, TOK), 0)
        earlier = ones_where(iota((TOK, TOK), 0) <= iota((TOK, TOK), 1))
        ids_row = jnp.broadcast_to(rows_ref[pl.ds(index, 1), :TOK], (16, TOK))
        hit = ones_where(ids_row == (slot // 2).astype(jnp.float32))
        rank = dot(hit, earlier)
        return ones_where((hit > 0) & (rank == (slot % 2 + 1).astype(jnp.float32)))

    def packing(rows_ref, index, which, m):
        wide = dot(slots(rows_ref, index), spread).astype(jnp.bfloat16)
        pack_m[which, m] = dot(to_row, wide).astype(jnp.bfloat16) * mask[...]

    def dispatch_copy(m, zz, to):
        return pltpu.make_async_remote_copy(
            src_ref=sent.at[m, zz],
            dst_ref=landed.at[m, z],
            send_sem=sent_sem.at[m, zz],
            recv_sem=landed_sem.at[m, z],
            device_id=at(to, zz, y, c),
            device_id_type=MESH,
        )

    def own_copy(m):
        return pltpu.make_async_copy(sent.at[m, z], landed.at[m, z], landed_sem.at[m, z])

    def pack(which, m):
        sent[m] = (
            dot(pack_m[which, m], state[m]).astype(jnp.bfloat16).reshape(Z, 16, PIECE)
        )

    def dispatch(m, to):
        each(Z - 1, lambda i: dispatch_copy(m, (z + far(i)) % Z, to).start())

        @pl.when(to == x)
        def _():
            own_copy(m).start()

        @pl.when(to != x)
        def _():
            dispatch_copy(m, z, to).start()

    def dispatch_sent(m, to):
        each(Z - 1, lambda i: dispatch_copy(m, (z + far(i)) % Z, to).wait_send())

        @pl.when(to != x)
        def _():
            dispatch_copy(m, z, to).wait_send()

    @pl.when(x == 0)
    def _():
        each(MB, lambda m: packing(ids_own, m, 0, m))
        each(MB * pieces, lambda i: token_load(i // pieces, i % pieces).wait())
        each(MB, lambda m: pack(0, m))

    @pl.when((x == 0) | (x == segments - 1))
    def _():
        pl.semaphore_wait(barrier, 11 + Z)

    @pl.when((x > 0) & (x < segments - 1))
    def _():
        pl.semaphore_wait(barrier, 11 + 2 * Z)

    @pl.when(x == 0)
    def _():
        each(MB, lambda m: dispatch(m, 0))

    ids_copy = pltpu.make_async_remote_copy(
        src_ref=ids_own,
        dst_ref=ids_next,
        send_sem=ids_sem.at[0],
        recv_sem=ids_sem.at[1],
        device_id=at(jnp.maximum(x - 1, 0), z, y, c),
        device_id_type=MESH,
    )

    @pl.when(x > 0)
    def _():
        ids_copy.start()

    p_row, p_col = iota((128, 128), 0), iota((128, 128), 1)
    perm[...] = ones_where(
        (p_col == ((p_row // 2) % 8) * 16 + (p_row // 16) * 2 + p_row % 2)
        & ((p_row // 2) % 8 < pieces)
    )
    perm_t[...] = ones_where(
        (p_row == ((p_col // 2) % 8) * 16 + (p_col // 16) * 2 + p_col % 2)
        & ((p_col // 2) % 8 < pieces)
    )
    each(MB, lambda m: packing(ids_own, MB + m, 1, m))

    eye = jnp.where(iota((TOK, TOK), 0) == iota((TOK, TOK), 1), 1.0, 0.0)
    transposed = (((1,), (1,)), ((), ()))
    scale_col = lax.dot_general(
        eye,
        scale_ref[...],
        transposed,
        precision=lax.Precision.HIGHEST,
        preferred_element_type=jnp.float32,
    )
    for i in range(LMAX * MB):
        scale_cols[i] = jnp.broadcast_to(scale_col[:, i : i + 1], (TOK, 128))
    from_slot = ones_where((iota((16, 128), 1) // 16) * 2 + iota((16, 128), 1) % 2 == iota((16, 128), 0))
    column_j = (iota((TOK, 128), 1) // 2) % 8

    def unpacking(i):
        turned = lax.dot_general(
            eye.astype(jnp.bfloat16),
            slots(ids_own, i),
            transposed,
            preferred_element_type=jnp.float32,
        )
        wide = dot(turned.astype(jnp.bfloat16), from_slot)
        for j in range(pieces):
            unpack_m[i, j * TOK : (j + 1) * TOK] = jnp.where(column_j == j, wide, 0.0).astype(
                jnp.bfloat16
            )

    each(LMAX * MB, unpacking)

    @pl.when(x < segments - 1)
    def _():
        ids_copy.wait_recv()
        each(MB, lambda m: packing(ids_next, m, 2, m))

    @pl.when(x > 0)
    def _():
        ids_copy.wait_send()

    for layer in range(LMAX):
        for i in range(3):
            weight_load(layer, i).wait()

    def section_of(k):
        total = jnp.int32(0)
        for start in starts[1:]:
            total = total + jnp.where(k >= start, 1, 0)
        return total

    def layer_of(k):
        total = k
        for before, start in zip(starts[:-1], starts[1:]):
            total = total - jnp.where(k >= start, start - before, 0)
        return total

    def state_copy(m):
        return pltpu.make_async_remote_copy(
            src_ref=state.at[m],
            dst_ref=state.at[m],
            send_sem=state_sem.at[0, m],
            recv_sem=state_sem.at[1, m],
            device_id=at(jnp.minimum(x + 1, segments - 1), z, y, c),
            device_id_type=MESH,
        )

    mine = c * Y + y

    def gather_copy(m, d):
        return pltpu.make_async_remote_copy(
            src_ref=gathered.at[m, mine],
            dst_ref=gathered.at[m, mine],
            send_sem=gather_send_sem.at[m, d],
            recv_sem=gather_sem.at[m, mine],
            device_id=at(x, z, (y + d) % Y, c),
            device_id_type=MESH,
        )

    def forward(m, yy):
        block = c * Y + yy
        return pltpu.make_async_remote_copy(
            src_ref=gathered.at[m, block],
            dst_ref=gathered.at[m, block],
            send_sem=gather_send_sem.at[m, 4 + yy],
            recv_sem=gather_sem.at[m, block],
            device_id=at(x, z, y, 1 - c),
            device_id_type=MESH,
        )

    def arrived(m, block):
        pltpu.make_async_copy(
            gathered.at[m, block], gathered.at[m, block], gather_sem.at[m, block]
        ).wait()

    def relay(m, layer):
        each(
            Z,
            lambda zz: pltpu.make_async_copy(
                landed.at[m, zz], landed.at[m, zz], landed_sem.at[m, zz]
            ).wait(),
        )
        rows = dot(perm_t[...], landed[m].reshape(128, PIECE))
        square = jnp.zeros((16, 1), jnp.float32)
        for j in range(pieces):
            piece = rows[16 * j : 16 * j + 16]
            square = square + jnp.sum(piece * piece, axis=1, keepdims=True)
        ratio = lax.rsqrt(square / width + 1e-06)
        gain = gain_ref[0, pl.ds(layer, 1), :]
        for j in range(pieces):
            span = slice(j * PIECE, (j + 1) * PIECE)
            gathered[m, mine, :, span] = (
                rows[16 * j : 16 * j + 16] * ratio * gain[:, span]
            ).astype(jnp.bfloat16)
        each(Y - 1, lambda i: gather_copy(m, (i + 1) % 3 + 1).start())
        forward(m, y).start()

    def pass_on(m):
        def one(i):
            yy = (y + 1 + 2 * i - 3 * (i // 2)) % Y
            arrived(m, c * Y + yy)
            forward(m, yy).start()

        each(Y - 1, one)

    def sibling_copy(m, yy):
        return pltpu.make_async_remote_copy(
            src_ref=part.at[m, 1 - c, yy],
            dst_ref=sibling_part.at[m, yy],
            send_sem=sib_sem.at[0, m, yy],
            recv_sem=sib_sem.at[1, m, yy],
            device_id=at(x, z, y, 1 - c),
            device_id_type=MESH,
        )

    def experts(m, layer):
        each(Y, lambda yy: arrived(m, (1 - c) * Y + yy))

        half = width // 2

        def hidden_part(i):
            span = pl.ds(pl.multiple_of(i * half, 256), half)
            rows = gathered[m, :, :, span].reshape(128, half)
            both[0] += dot(rows, gate_w[layer, span, :])
            both[1] += dot(rows, up_w[layer, span, :])

        both[...] = jnp.zeros_like(both)
        each(2, hidden_part)
        gate, up = both[0], both[1]
        hidden = (gate * lax.logistic(gate) * up).astype(jnp.bfloat16)


        def output_part(i):
            span = pl.ds(pl.multiple_of(i * half, 256), half)
            part[m, :, :, :, span] = (
                dot(hidden, down_w[layer, :, span]).astype(jnp.bfloat16).reshape(2, Y, 16, half)
            )

        each(2, output_part)
        each(Y, lambda i: sibling_copy(m, (y + 2 + i) % Y).start())

    def reduce_copy(m, d):
        return pltpu.make_async_remote_copy(
            src_ref=pair.at[m, (y + d) % Y],
            dst_ref=reduced.at[m, y],
            send_sem=reduce_send_sem.at[m, d],
            recv_sem=reduce_sem.at[m, y],
            device_id=at(x, z, (y + d) % Y, c),
            device_id_type=MESH,
        )

    def chip_sum(m):
        each(Y - 1, lambda i: gather_copy(m, i + 1).wait_send())
        each(Y, lambda i: forward(m, i).wait_send())

        def one(i):
            d = (2 + i) % Y
            yy = (y + d) % Y
            sibling_copy(m, yy).wait_recv()
            pair[m, yy] = (
                part[m, c, yy].astype(jnp.float32) + sibling_part[m, yy].astype(jnp.float32)
            ).astype(jnp.bfloat16)

            @pl.when(d > 0)
            def _():
                reduce_copy(m, d).start()

        each(Y, one)

    def back_copy(m, zz):
        return pltpu.make_async_remote_copy(
            src_ref=back.at[m, zz],
            dst_ref=returned.at[m, z],
            send_sem=back_sem.at[m, zz],
            recv_sem=returned_sem.at[m, z],
            device_id=at(x, zz, y, c),
            device_id_type=MESH,
        )

    def own_back(m):
        return pltpu.make_async_copy(back.at[m, z], returned.at[m, z], returned_sem.at[m, z])

    def plane_sum(m):
        def one(i):
            yy = (y + i + 1) % Y
            pltpu.make_async_copy(
                reduced.at[m, yy], reduced.at[m, yy], reduce_sem.at[m, yy]
            ).wait()

        each(Y - 1, one)
        total = []
        for j in range(pieces):
            span = slice(j * PIECE, (j + 1) * PIECE)
            value = pair[m, y, :, span].astype(jnp.float32)
            for d in range(1, Y):
                value = value + reduced[m, (y + d) % Y, :, span].astype(jnp.float32)
            total.append(value.astype(jnp.bfloat16))
        stacked = jnp.concatenate(total, axis=0)
        back[m] = (
            dot(perm[:, : 16 * pieces], stacked).astype(jnp.bfloat16).reshape(Z, 16, PIECE)
        )
        each(Z - 1, lambda i: back_copy(m, (z + far(i)) % Z).start())
        own_back(m).start()

    def combine(m, layer):
        each(
            Z,
            lambda zz: pltpu.make_async_copy(
                returned.at[m, zz], returned.at[m, zz], returned_sem.at[m, zz]
            ).wait(),
        )
        values = returned[m].reshape(128, PIECE)
        column = scale_cols[layer * MB + m][:, :1]

        def one(j):
            span = pl.ds(pl.multiple_of(j * TOK, TOK), TOK)
            picked = dot(unpack_m[layer * MB + m, span], values)
            before = state[m, span].astype(jnp.float32)
            state[m, span] = (before + column * picked).astype(jnp.bfloat16)

        each(pieces, one)

    def finish(m):
        each(Y, lambda i: sibling_copy(m, i).wait_send())
        each(Y - 1, lambda i: reduce_copy(m, i + 1).wait_send())
        each(Z - 1, lambda i: back_copy(m, (z + far(i)) % Z).wait_send())

    def close(m, k, section, layer):
        after = section_of(k + 1)

        @pl.when((layer == 0) & (section > 0))
        def _():
            pltpu.make_async_copy(state.at[m], state.at[m], state_sem.at[1, m]).wait()

        combine(m, layer)

        @pl.when((layer > 0) | (section == 0))
        def _():
            dispatch_sent(m, x)

        @pl.when(k + 1 < steps)
        def _():
            pack(jnp.where(after != section, 2, 1), m)
            dispatch(m, after)

        @pl.when((k + 1 < steps) & (after != section))
        def _():
            state_copy(m).start()

        finish(m)

    def slot_of_step(u, carry):
        k, u = u // 4, u % 4
        k_late = jnp.where(u == 0, k - 1, k)
        section, layer = section_of(k), layer_of(k)
        section_late, layer_late = section_of(k_late), layer_of(k_late)
        now = (x == section) & (k < steps)
        late = (x == section_late) & (k_late >= 0) & (k_late < steps)
        lagging = jnp.where(u == 0, 1, 0)

        @pl.when(now & ((u == 0) | (u == 2)))
        def _():
            relay(u // 2, layer)

        @pl.when(late & (u < 2))
        def _():
            plane_sum(lagging)

        @pl.when(now & ((u == 0) | (u == 3)))
        def _():
            m = u // 3
            pass_on(m)
            experts(m, layer)
            chip_sum(m)

        @pl.when(late & ((u == 0) | (u == 2)))
        def _():
            close(lagging, k_late, section_late, layer_late)

        return carry

    lax.fori_loop(0, 4 * steps + 1, slot_of_step, 0)

    def write_out(i):
        m, j = i // pieces, i % pieces
        span = pl.ds(pl.multiple_of(j * PIECE, PIECE), PIECE)
        out_ref[0, m, :, span] = state[m, pl.ds(pl.multiple_of(j * TOK, TOK), TOK)]

    each(MB * pieces, write_out)

    @pl.when(x < segments - 1)
    def _():
        for m in range(MB):
            state_copy(m).wait_send()
            dispatch_sent(m, x + 1)


def run(depths_static, collective, args):
    tokens, gain, gate, up, down, ids, scale = args
    starts, total = [], 0
    for d in depths_static:
        starts.append(total)
        total += d
    width = tokens.shape[2]
    hidden = gate.shape[3]
    pieces = width // PIECE
    lanes = pieces * TOK
    vmem = pl.BlockSpec(memory_space=pltpu.VMEM)
    hbm = pl.BlockSpec(memory_space=pl.ANY)
    bf = jnp.bfloat16
    dma = pltpu.SemaphoreType.DMA
    return pl.pallas_call(
        functools.partial(kernel, tuple(starts), total),
        out_shape=jax.ShapeDtypeStruct((1, MB, TOK, width), bf),
        in_specs=[hbm, vmem, hbm, hbm, hbm, vmem, vmem],
        out_specs=vmem,
        scratch_shapes=[
            pltpu.VMEM((LMAX, width, hidden), bf),
            pltpu.VMEM((LMAX, width, hidden), bf),
            pltpu.VMEM((LMAX, hidden, width), bf),
            pltpu.VMEM((MB, lanes, PIECE), bf),
            pltpu.VMEM((8, 128), jnp.float32),
            pltpu.VMEM((8, 128), jnp.float32),
            pltpu.VMEM((LMAX * MB, TOK, 128), jnp.float32),
            pltpu.VMEM((128, lanes), bf),
            pltpu.VMEM((3, MB, 128, lanes), bf),
            pltpu.VMEM((LMAX * MB, lanes, 128), bf),
            pltpu.VMEM((128, 128), bf),
            pltpu.VMEM((128, 128), bf),
            pltpu.VMEM((2, 128, hidden), jnp.float32),
            pltpu.VMEM((MB, Z, 16, PIECE), bf),
            pltpu.VMEM((MB, Z, 16, PIECE), bf),
            pltpu.VMEM((MB, 8, 16, width), bf),
            pltpu.VMEM((MB, 2, Y, 16, width), bf),
            pltpu.VMEM((MB, Y, 16, width), bf),
            pltpu.VMEM((MB, Y, 16, width), bf),
            pltpu.VMEM((MB, Y, 16, width), bf),
            pltpu.VMEM((MB, Z, 16, PIECE), bf),
            pltpu.VMEM((MB, Z, 16, PIECE), bf),
            dma((MB, pieces)),
            dma((LMAX, 3)),
            dma((2, MB)),
            dma((2,)),
            dma((MB, Z)),
            dma((MB, Z)),
            dma((MB, 8)),
            dma((MB, 8)),
            dma((2, MB, Y)),
            dma((MB, Y)),
            dma((MB, Y)),
            dma((MB, Z)),
            dma((MB, Z)),
        ],
        compiler_params=pltpu.CompilerParams(
            collective_id=collective, has_side_effects=True, vmem_limit_bytes=48 * 2**20
        ),
        name="relay_layers",
    )(tokens, gain, gate, up, down, ids, scale)


def depth_kernel(depth_ref, out_ref, mine, send_sem, recv_sem):
    x = lax.axis_index("segment")
    me = lax.axis_index("expert")
    segments = lax.axis_size("segment")
    barrier = pltpu.get_barrier_semaphore()
    for d in range(1, segments):
        pl.semaphore_signal(
            barrier, inc=1, device_id=((x + d) % segments, me), device_id_type=MESH
        )
    mine[...] = jnp.broadcast_to(depth_ref[0], (8, 128))
    out_ref[x] = jnp.broadcast_to(depth_ref[0], (8, 128))
    pl.semaphore_wait(barrier, segments - 1)
    copies = []
    for d in range(1, segments):
        copy = pltpu.make_async_remote_copy(
            src_ref=mine,
            dst_ref=out_ref.at[x],
            send_sem=send_sem.at[d],
            recv_sem=recv_sem.at[x],
            device_id=((x + d) % segments, me),
            device_id_type=MESH,
        )
        copy.start()
        copies.append(copy)
    for d in range(1, segments):
        other = (x + d) % segments
        pltpu.make_async_copy(out_ref.at[other], out_ref.at[other], recv_sem.at[other]).wait()
    for copy in copies:
        copy.wait_send()


def depth_exchange(depths):
    vmem = pl.BlockSpec(memory_space=pltpu.VMEM)
    return pl.pallas_call(
        depth_kernel,
        out_shape=jax.ShapeDtypeStruct((4, 8, 128), jnp.int32),
        in_specs=[pl.BlockSpec(memory_space=pltpu.SMEM)],
        out_specs=vmem,
        scratch_shapes=[
            pltpu.VMEM((8, 128), jnp.int32),
            pltpu.SemaphoreType.DMA((4,)),
            pltpu.SemaphoreType.DMA((4,)),
        ],
        compiler_params=pltpu.CompilerParams(collective_id=0, has_side_effects=True),
        name="share_depths",
    )(depths)


def local(tokens, norm_gain, gate_weight, up_weight, down_weight, expert_ids, gate_scale, depths):
    args = (
        tokens,
        norm_gain,
        gate_weight,
        up_weight,
        down_weight,
        expert_ids.reshape(LMAX * MB, TOK),
        gate_scale.reshape(LMAX * MB, TOK),
    )
    every = depth_exchange(depths)[:, 0, 0]
    code = jnp.sum((every > 1).astype(jnp.int32) * jnp.asarray([1, 2, 4, 8], jnp.int32))
    branches = []
    for number in range(1, 15):
        pattern = tuple(1 + (number >> s) % 2 for s in range(4))
        branches.append(functools.partial(run, pattern, number))
    return lax.switch(code - 1, branches, args)


def solution(mesh):
    return jax.shard_map(
        local,
        mesh=mesh,
        in_specs=(
            P(None, "expert", None),
            P("segment", None, None),
            P("segment", None, None, "expert"),
            P("segment", None, None, "expert"),
            P("segment", None, "expert", None),
            P("segment", None, None, "expert"),
            P("segment", None, None, "expert"),
            P("segment"),
        ),
        out_specs=P("segment", None, "expert", None),
        check_vma=False,
    )
```

time: 293 us -> 223 us (0.76)
  Pallas kernels: 285 us -> 218 us
  local copies, waits for them, and re-layouts: 7.2 us -> 0.93 us
    pallas_call x1, Pallas kernels: 285 us -> 212 us  [run(): pl.pallas_call(functools.partial(kernel, tuple(starts), total), out_shape...]
    pallas_call x0 -> x1, Pallas kernels: none -> 6.09 us  [depth_exchange(): pl.pallas_call(depth_kernel, out_shape=jax.ShapeDtypeStruct((4, 8, 128),...]
    unnamed x7 -> x1, local copies, waits for them, and re-layouts: 4.89 us -> 0.93 us
where the time goes in v2:
time: 223 us; the launch traced here: 222 us
  Pallas kernels  218 us (98%)
    pallas_call x1, Pallas kernels, run(): pl.pallas_call(functools.partial(kernel, tuple(starts), total), out_shape...  212 us
    pallas_call x1, Pallas kernels, depth_exchange(): pl.pallas_call(depth_kernel, out_shape=jax.ShapeDtypeStruct((4, 8, 128),...  6.09 us

profile of v2, /device:TPU:6, one launch (start us, length us, event | category | flops | bytes accessed | tf_op | source)
XLA Modules:
  0.0 222.3 jit_solution(4816100817830874204)
XLA Ops:
  0.7 6.1 %share_depths.1 = s32[4,8,128]{2,1,0:T(8,128)} custom-call(s32[1]{0:T(128)S(6)} %copy.39.depth_ref), custom_call_target="tpu_custom_call" | custom-call | tf_op jit(solution)/shard_map/share_depths/pallas_call | solution.py:641
  6.7 1.4 fusion
  8.8 212.6 %conditional.1 = (bf16[1,2,64,3584]{3,2,1,0:T(8,128)(2,1)S(1)}) conditional(s32[]{:T(128)} %clamp.3, (bf16[2,64,3584]{2,1,0:T(8,128)(2,1)}, f32[1,2,3584]{2,1,0:T(2,128)}, bf16[1,2,3584,256]{3,2,1,0:T(8,128)(2,1)}, bf16[1,2,3584,256]{3,2,1,0:T(8,128)(2,1)}, bf16[1,2,256,3584]{3,2,1,0:T(8,128)(2,1)}, ...), branch_computations={%region_1.0_spmd, %region_2.0_spmd, %region_3.0_spmd, %region_4.0_... | conditional | bytes 8 | solution.py:672
  9.0 211.9 %relay_layers.19 = bf16[1,2,64,3584]{3,2,1,0:T(8,128)(2,1)S(1)} custom-call(bf16[2,64,3584]{2,1,0:T(8,128)(2,1)} %get-tuple-element.251.tokens_hbm, f32[1,2,3584]{2,1,0:T(2,128)} %get-tuple-element.252.gain_ref, bf16[1,2,3584,256]{3,2,1,0:T(8,128)(2,1)} %get-tuple-element.253.gate_hbm, bf16[1,2,3584,256]{3,2,1,0:T(8,128)(2,1)} %get-tuple-element.254.up_hbm, ...), custom_call_target="tpu_custom_call" | custom-call | tf_op jit(solution)/shard_map/cond/branch_5_fun/relay_layers/pallas_call | solution.py:559
  221.4 0.9 copy.40

commit v3 on v2

--- a/solution.py
+++ b/solution.py
@@ -38,14 +38,17 @@
     down_hbm,
     ids_ref,
     scale_ref,
-    out_ref,
-    gate_w,
-    up_w,
+    depth_ref,
+    out_hbm,
+    in_w,
     down_w,
     state,
-    ids_own,
-    ids_next,
+    all_ids,
     scale_cols,
+    scale_rows,
+    base,
+    link,
+    link_scale,
     mask,
     pack_m,
     unpack_m,
@@ -62,6 +65,7 @@
     back,
     returned,
     token_sem,
+    out_sem,
     weight_sem,
     state_sem,
     ids_sem,
@@ -94,17 +98,22 @@
     def far(i):
         return 4 + ((i + 1) // 2) * (1 - 2 * (i % 2))
 
+    def chip_order(i):
+        return jnp.where(i < 2, 2 + i, 3 - i)
+
     def weight_load(layer, i):
-        src, dst = ((gate_hbm, gate_w), (up_hbm, up_w), (down_hbm, down_w))[i]
+        src, dst = ((gate_hbm, in_w.at[0]), (up_hbm, in_w.at[1]), (down_hbm, down_w))[i]
         return pltpu.make_async_copy(src.at[0, layer], dst.at[layer], weight_sem.at[layer, i])
 
     def token_load(m, j):
         return pltpu.make_async_copy(
-            tokens_hbm.at[m, :, pl.ds(j * PIECE, PIECE)],
-            state.at[m, pl.ds(j * TOK, TOK)],
+            tokens_hbm.at[m, :, pl.ds(pl.multiple_of(j * PIECE, PIECE), PIECE)],
+            state.at[m, pl.ds(pl.multiple_of(j * TOK, TOK), TOK)],
             token_sem.at[m, j],
         )
 
+    all_ids[...] = jnp.zeros_like(all_ids)
+    all_ids[0 : LMAX * MB, :TOK] = ids_ref[...].astype(jnp.float32)
     barrier = pltpu.get_barrier_semaphore()
 
     def greet(device):
@@ -114,40 +123,38 @@
     each(Y - 1, lambda i: greet(at(x, z, (y + i + 1) % Y, c)))
     greet(at(x, z, y, 1 - c))
 
-    @pl.when(x > 0)
-    def _():
-        each(Z, lambda i: greet(at(x - 1, (z + i) % Z, y, c)))
-
-    @pl.when(x < segments - 1)
-    def _():
-        each(Z, lambda i: greet(at(x + 1, (z + i) % Z, y, c)))
+    def greet_beside(i):
+        beside = x - 1 + 2 * (i // Z)
+
+        @pl.when((beside >= 0) & (beside < segments))
+        def _():
+            greet(at(beside, (z + i) % Z, y, c))
+
+    each(2 * Z, greet_beside)
 
     @pl.when(x == 0)
     def _():
         each(MB * pieces, lambda i: token_load(i // pieces, i % pieces).start())
 
-    for layer in range(LMAX):
-        for i in range(3):
-            weight_load(layer, i).start()
+    for i in range(3):
+        each(LMAX, lambda layer: weight_load(layer, i).start())
 
     lanes = pieces * TOK
     spread = ones_where(iota((TOK, lanes), 0) == iota((TOK, lanes), 1) % TOK)
     row_slot = iota((128, 16), 0)
     to_row = ones_where((row_slot // 16) * 2 + row_slot % 2 == iota((128, 16), 1))
     mask[...] = ones_where((iota((128, lanes), 0) // 2) % 8 == iota((128, lanes), 1) // TOK)
-    ids_own[...] = jnp.zeros_like(ids_own)
-    ids_own[0 : LMAX * MB, :TOK] = ids_ref[...].astype(jnp.float32)
-
-    def slots(rows_ref, index):
+
+    def slots(index):
         slot = iota((16, TOK), 0)
         earlier = ones_where(iota((TOK, TOK), 0) <= iota((TOK, TOK), 1))
-        ids_row = jnp.broadcast_to(rows_ref[pl.ds(index, 1), :TOK], (16, TOK))
+        ids_row = jnp.broadcast_to(all_ids[pl.ds(index, 1), :TOK], (16, TOK))
         hit = ones_where(ids_row == (slot // 2).astype(jnp.float32))
         rank = dot(hit, earlier)
         return ones_where((hit > 0) & (rank == (slot % 2 + 1).astype(jnp.float32)))
 
-    def packing(rows_ref, index, which, m):
-        wide = dot(slots(rows_ref, index), spread).astype(jnp.bfloat16)
+    def packing(index, which, m):
+        wide = dot(slots(index), spread).astype(jnp.bfloat16)
         pack_m[which, m] = dot(to_row, wide).astype(jnp.bfloat16) * mask[...]
 
     def dispatch_copy(m, zz, to):
@@ -169,26 +176,30 @@
         )
 
     def dispatch(m, to):
-        each(Z - 1, lambda i: dispatch_copy(m, (z + far(i)) % Z, to).start())
+        def one(i):
+            zz = (z + far(i)) % Z
+
+            @pl.when((zz != z) | (to != x))
+            def _():
+                dispatch_copy(m, zz, to).start()
+
+        each(Z, one)
 
         @pl.when(to == x)
         def _():
             own_copy(m).start()
 
-        @pl.when(to != x)
-        def _():
-            dispatch_copy(m, z, to).start()
-
     def dispatch_sent(m, to):
-        each(Z - 1, lambda i: dispatch_copy(m, (z + far(i)) % Z, to).wait_send())
-
-        @pl.when(to != x)
-        def _():
-            dispatch_copy(m, z, to).wait_send()
+        def one(zz):
+            @pl.when((zz != z) | (to != x))
+            def _():
+                dispatch_copy(m, zz, to).wait_send()
+
+        each(Z, one)
 
     @pl.when(x == 0)
     def _():
-        each(MB, lambda m: packing(ids_own, m, 0, m))
+        each(MB, lambda m: packing(m, 0, m))
         each(MB * pieces, lambda i: token_load(i // pieces, i % pieces).wait())
         each(MB, lambda m: pack(0, m))
 
@@ -205,8 +216,8 @@
         each(MB, lambda m: dispatch(m, 0))
 
     ids_copy = pltpu.make_async_remote_copy(
-        src_ref=ids_own,
-        dst_ref=ids_next,
+        src_ref=all_ids.at[0:8],
+        dst_ref=all_ids.at[8:16],
         send_sem=ids_sem.at[0],
         recv_sem=ids_sem.at[1],
         device_id=at(jnp.maximum(x - 1, 0), z, y, c),
@@ -226,49 +237,63 @@
         (p_row == ((p_col // 2) % 8) * 16 + (p_col // 16) * 2 + p_col % 2)
         & ((p_col // 2) % 8 < pieces)
     )
-    each(MB, lambda m: packing(ids_own, MB + m, 1, m))
-
+
+    scale = jnp.where(iota((LMAX * MB, TOK), 0) // MB < depth_ref[0], scale_ref[...], 0.0)
     eye = jnp.where(iota((TOK, TOK), 0) == iota((TOK, TOK), 1), 1.0, 0.0)
     transposed = (((1,), (1,)), ((), ()))
     scale_col = lax.dot_general(
         eye,
-        scale_ref[...],
+        scale,
         transposed,
+        precision=lax.Precision.HIGHEST,
+        preferred_element_type=jnp.float32,
+    )
+    scale_rows[0 : LMAX * MB] = jnp.dot(
+        scale,
+        spread.astype(jnp.float32),
         precision=lax.Precision.HIGHEST,
         preferred_element_type=jnp.float32,
     )
     for i in range(LMAX * MB):
         scale_cols[i] = jnp.broadcast_to(scale_col[:, i : i + 1], (TOK, 128))
+
     from_slot = ones_where((iota((16, 128), 1) // 16) * 2 + iota((16, 128), 1) % 2 == iota((16, 128), 0))
     column_j = (iota((TOK, 128), 1) // 2) % 8
 
     def unpacking(i):
         turned = lax.dot_general(
             eye.astype(jnp.bfloat16),
-            slots(ids_own, i),
+            slots(i),
             transposed,
             preferred_element_type=jnp.float32,
         )
         wide = dot(turned.astype(jnp.bfloat16), from_slot)
-        for j in range(pieces):
-            unpack_m[i, j * TOK : (j + 1) * TOK] = jnp.where(column_j == j, wide, 0.0).astype(
-                jnp.bfloat16
-            )
+
+        def piece(j):
+            unpack_m[i, pl.ds(pl.multiple_of(j * TOK, TOK), TOK)] = jnp.where(
+                column_j == j, wide, 0.0
+            ).astype(jnp.bfloat16)
+
+        each(pieces, piece)
 
     each(LMAX * MB, unpacking)
 
     @pl.when(x < segments - 1)
     def _():
         ids_copy.wait_recv()
-        each(MB, lambda m: packing(ids_next, m, 2, m))
+
+    def packing_later(i):
+        m = i % MB
+        packing(jnp.where(i < MB, MB + m, 8 + m), 1 + i // MB, m)
+
+    each(2 * MB, packing_later)
 
     @pl.when(x > 0)
     def _():
         ids_copy.wait_send()
 
-    for layer in range(LMAX):
-        for i in range(3):
-            weight_load(layer, i).wait()
+    for i in range(3):
+        each(LMAX, lambda layer: weight_load(layer, i).wait())
 
     def section_of(k):
         total = jnp.int32(0)
@@ -368,8 +393,8 @@
         def hidden_part(i):
             span = pl.ds(pl.multiple_of(i * half, 256), half)
             rows = gathered[m, :, :, span].reshape(128, half)
-            both[0] += dot(rows, gate_w[layer, span, :])
-            both[1] += dot(rows, up_w[layer, span, :])
+            both[0] += dot(rows, in_w[0, layer, span, :])
+            both[1] += dot(rows, in_w[1, layer, span, :])
 
         both[...] = jnp.zeros_like(both)
         each(2, hidden_part)
@@ -384,7 +409,7 @@
             )
 
         each(2, output_part)
-        each(Y, lambda i: sibling_copy(m, (y + 2 + i) % Y).start())
+        each(Y, lambda i: sibling_copy(m, (y + chip_order(i)) % Y).start())
 
     def reduce_copy(m, d):
         return pltpu.make_async_remote_copy(
@@ -401,7 +426,7 @@
         each(Y, lambda i: forward(m, i).wait_send())
 
         def one(i):
-            d = (2 + i) % Y
+            d = chip_order(i)
             yy = (y + d) % Y
             sibling_copy(m, yy).wait_recv()
             pair[m, yy] = (
@@ -450,45 +475,66 @@
         own_back(m).start()
 
     def combine(m, layer):
+        values = returned[m].reshape(128, PIECE)
+        column = scale_cols[layer * MB + m][:, :1]
+
+        def one(j):
+            span = pl.ds(pl.multiple_of(j * TOK, TOK), TOK)
+            picked = dot(unpack_m[layer * MB + m, span], values)
+            before = state[m, span].astype(jnp.float32)
+            state[m, span] = (before + column * picked).astype(jnp.bfloat16)
+
+        each(pieces, one)
+
+    def prepare(m, layer, which):
+        rows = pack_m[which, m]
+        base[...] = dot(rows, state[m])
+        link[...] = dot(rows, unpack_m[layer * MB + m]).astype(jnp.bfloat16)
+        scales = jnp.sum(
+            rows.astype(jnp.float32) * scale_rows[pl.ds(layer * MB + m, 1), :],
+            axis=1,
+            keepdims=True,
+        )
+        link_scale[...] = jnp.broadcast_to(scales, (128, 128))
+
+    def finish(m):
+        each(Y, lambda i: sibling_copy(m, i).wait_send())
+        each(Y - 1, lambda i: reduce_copy(m, i + 1).wait_send())
+        each(Z - 1, lambda i: back_copy(m, (z + far(i)) % Z).wait_send())
+
+    def close(m, k, section, layer):
+        after = section_of(k + 1)
+
+        @pl.when((layer == 0) & (section > 0))
+        def _():
+            pltpu.make_async_copy(state.at[m], state.at[m], state_sem.at[1, m]).wait()
+
+        @pl.when((layer > 0) | (section == 0))
+        def _():
+            dispatch_sent(m, x)
+
+        @pl.when(k + 1 < steps)
+        def _():
+            prepare(m, layer, jnp.where(after != section, 2, 1))
+
         each(
             Z,
             lambda zz: pltpu.make_async_copy(
                 returned.at[m, zz], returned.at[m, zz], returned_sem.at[m, zz]
             ).wait(),
         )
-        values = returned[m].reshape(128, PIECE)
-        column = scale_cols[layer * MB + m][:, :1]
-
-        def one(j):
-            span = pl.ds(pl.multiple_of(j * TOK, TOK), TOK)
-            picked = dot(unpack_m[layer * MB + m, span], values)
-            before = state[m, span].astype(jnp.float32)
-            state[m, span] = (before + column * picked).astype(jnp.bfloat16)
-
-        each(pieces, one)
-
-    def finish(m):
-        each(Y, lambda i: sibling_copy(m, i).wait_send())
-        each(Y - 1, lambda i: reduce_copy(m, i + 1).wait_send())
-        each(Z - 1, lambda i: back_copy(m, (z + far(i)) % Z).wait_send())
-
-    def close(m, k, section, layer):
-        after = section_of(k + 1)
-
-        @pl.when((layer == 0) & (section > 0))
-        def _():
-            pltpu.make_async_copy(state.at[m], state.at[m], state_sem.at[1, m]).wait()
+
+        @pl.when(k + 1 < steps)
+        def _():
+            result = dot(link[...], returned[m].reshape(128, PIECE))
+            sent[m] = (
+                (base[...] + link_scale[:, :1] * result)
+                .astype(jnp.bfloat16)
+                .reshape(Z, 16, PIECE)
+            )
+            dispatch(m, after)
 
         combine(m, layer)
-
-        @pl.when((layer > 0) | (section == 0))
-        def _():
-            dispatch_sent(m, x)
-
-        @pl.when(k + 1 < steps)
-        def _():
-            pack(jnp.where(after != section, 2, 1), m)
-            dispatch(m, after)
 
         @pl.when((k + 1 < steps) & (after != section))
         def _():
@@ -530,20 +576,26 @@
 
     def write_out(i):
         m, j = i // pieces, i % pieces
-        span = pl.ds(pl.multiple_of(j * PIECE, PIECE), PIECE)
-        out_ref[0, m, :, span] = state[m, pl.ds(pl.multiple_of(j * TOK, TOK), TOK)]
-
-    each(MB * pieces, write_out)
+        return pltpu.make_async_copy(
+            state.at[m, pl.ds(pl.multiple_of(j * TOK, TOK), TOK)],
+            out_hbm.at[0, m, :, pl.ds(pl.multiple_of(j * PIECE, PIECE), PIECE)],
+            out_sem.at[m, j],
+        )
+
+    each(MB * pieces, lambda i: write_out(i).start())
+    each(MB * pieces, lambda i: write_out(i).wait())
+
+    def all_sent(m):
+        state_copy(m).wait_send()
+        dispatch_sent(m, x + 1)
 
     @pl.when(x < segments - 1)
     def _():
-        for m in range(MB):
-            state_copy(m).wait_send()
-            dispatch_sent(m, x + 1)
+        each(MB, all_sent)
 
 
 def run(depths_static, collective, args):
-    tokens, gain, gate, up, down, ids, scale = args
+    tokens, gain, gate, up, down, ids, scale, depth = args
     starts, total = [], 0
     for d in depths_static:
         starts.append(total)
@@ -559,16 +611,18 @@
     return pl.pallas_call(
         functools.partial(kernel, tuple(starts), total),
         out_shape=jax.ShapeDtypeStruct((1, MB, TOK, width), bf),
-        in_specs=[hbm, vmem, hbm, hbm, hbm, vmem, vmem],
-        out_specs=vmem,
+        in_specs=[hbm, vmem, hbm, hbm, hbm, vmem, vmem, pl.BlockSpec(memory_space=pltpu.SMEM)],
+        out_specs=hbm,
         scratch_shapes=[
-            pltpu.VMEM((LMAX, width, hidden), bf),
-            pltpu.VMEM((LMAX, width, hidden), bf),
+            pltpu.VMEM((2, LMAX, width, hidden), bf),
             pltpu.VMEM((LMAX, hidden, width), bf),
             pltpu.VMEM((MB, lanes, PIECE), bf),
-            pltpu.VMEM((8, 128), jnp.float32),
-            pltpu.VMEM((8, 128), jnp.float32),
+            pltpu.VMEM((16, 128), jnp.float32),
             pltpu.VMEM((LMAX * MB, TOK, 128), jnp.float32),
+            pltpu.VMEM((8, lanes), jnp.float32),
+            pltpu.VMEM((128, PIECE), jnp.float32),
+            pltpu.VMEM((128, 128), bf),
+            pltpu.VMEM((128, 128), jnp.float32),
             pltpu.VMEM((128, lanes), bf),
             pltpu.VMEM((3, MB, 128, lanes), bf),
             pltpu.VMEM((LMAX * MB, lanes, 128), bf),
@@ -584,6 +638,7 @@
             pltpu.VMEM((MB, Y, 16, width), bf),
             pltpu.VMEM((MB, Z, 16, PIECE), bf),
             pltpu.VMEM((MB, Z, 16, PIECE), bf),
+            dma((MB, pieces)),
             dma((MB, pieces)),
             dma((LMAX, 3)),
             dma((2, MB)),
@@ -602,10 +657,10 @@
             collective_id=collective, has_side_effects=True, vmem_limit_bytes=48 * 2**20
         ),
         name="relay_layers",
-    )(tokens, gain, gate, up, down, ids, scale)
-
-
-def depth_kernel(depth_ref, out_ref, mine, send_sem, recv_sem):
+    )(tokens, gain, gate, up, down, ids, scale, depth)
+
+
+def depth_kernel(depth_ref, code_ref, mine, every, send_sem, recv_sem):
     x = lax.axis_index("segment")
     me = lax.axis_index("expert")
     segments = lax.axis_size("segment")
@@ -615,13 +670,13 @@
             barrier, inc=1, device_id=((x + d) % segments, me), device_id_type=MESH
         )
     mine[...] = jnp.broadcast_to(depth_ref[0], (8, 128))
-    out_ref[x] = jnp.broadcast_to(depth_ref[0], (8, 128))
+    every[x] = jnp.broadcast_to(depth_ref[0], (8, 128))
     pl.semaphore_wait(barrier, segments - 1)
     copies = []
-    for d in range(1, segments):
+    for d in (2, 1, 3):
         copy = pltpu.make_async_remote_copy(
             src_ref=mine,
-            dst_ref=out_ref.at[x],
+            dst_ref=every.at[x],
             send_sem=send_sem.at[d],
             recv_sem=recv_sem.at[x],
             device_id=((x + d) % segments, me),
@@ -629,28 +684,32 @@
         )
         copy.start()
         copies.append(copy)
-    for d in range(1, segments):
+    for d in (1, 3, 2):
         other = (x + d) % segments
-        pltpu.make_async_copy(out_ref.at[other], out_ref.at[other], recv_sem.at[other]).wait()
+        pltpu.make_async_copy(every.at[other], every.at[other], recv_sem.at[other]).wait()
+    code = jnp.zeros((8, 128), jnp.int32)
+    for s in range(4):
+        code = code + jnp.where(every[s] > 1, 1 << s, 0)
+    code_ref[0] = jnp.max(jnp.where(code == 1, 9, code)) - 2
     for copy in copies:
         copy.wait_send()
 
 
-def depth_exchange(depths):
-    vmem = pl.BlockSpec(memory_space=pltpu.VMEM)
+def pattern_of(depths):
     return pl.pallas_call(
         depth_kernel,
-        out_shape=jax.ShapeDtypeStruct((4, 8, 128), jnp.int32),
+        out_shape=jax.ShapeDtypeStruct((1,), jnp.int32),
         in_specs=[pl.BlockSpec(memory_space=pltpu.SMEM)],
-        out_specs=vmem,
+        out_specs=pl.BlockSpec(memory_space=pltpu.SMEM),
         scratch_shapes=[
             pltpu.VMEM((8, 128), jnp.int32),
+            pltpu.VMEM((4, 8, 128), jnp.int32),
             pltpu.SemaphoreType.DMA((4,)),
             pltpu.SemaphoreType.DMA((4,)),
         ],
         compiler_params=pltpu.CompilerParams(collective_id=0, has_side_effects=True),
         name="share_depths",
-    )(depths)
+    )(depths)[0]
 
 
 def local(tokens, norm_gain, gate_weight, up_weight, down_weight, expert_ids, gate_scale, depths):
@@ -662,14 +721,13 @@
         down_weight,
         expert_ids.reshape(LMAX * MB, TOK),
         gate_scale.reshape(LMAX * MB, TOK),
+        depths,
     )
-    every = depth_exchange(depths)[:, 0, 0]
-    code = jnp.sum((every > 1).astype(jnp.int32) * jnp.asarray([1, 2, 4, 8], jnp.int32))
     branches = []
-    for number in range(1, 15):
+    for number in range(2, 15):
         pattern = tuple(1 + (number >> s) % 2 for s in range(4))
         branches.append(functools.partial(run, pattern, number))
-    return lax.switch(code - 1, branches, args)
+    return lax.switch(pattern_of(depths), branches, args)
 
 
 def solution(mesh):

time: 223 us -> 218 us (0.978)
  Pallas kernels: 218 us -> 214 us
    pallas_call x1, Pallas kernels: 212 us -> 208 us  [run(): pl.pallas_call(functools.partial(kernel, tuple(starts), total), out_shape...]
where the time goes in v3:
time: 218 us; the launch traced here: 217 us
  Pallas kernels  214 us (98%)
    pallas_call x1, Pallas kernels, run(): pl.pallas_call(functools.partial(kernel, tuple(starts), total), out_shape...  208 us
    pallas_call x1, Pallas kernels, pattern_of(): pl.pallas_call(depth_kernel, out_shape=jax.ShapeDtypeStruct((1,), jnp.int...  6.21 us

profile of v3, /device:TPU:6, one launch (start us, length us, event | category | flops | bytes accessed | tf_op | source)
XLA Modules:
  0.0 217.2 jit_solution(6095547533625905586)
XLA Ops:
  0.7 6.2 %share_depths.1 = s32[1]{0:T(128)} custom-call(s32[1]{0:T(128)S(6)} %copy.36.depth_ref), custom_call_target="tpu_custom_call" | custom-call | tf_op jit(solution)/shard_map/share_depths/pallas_call | solution.py:699
  7.4 208.9 %conditional.1 = (bf16[1,2,64,3584]{3,2,1,0:T(8,128)(2,1)S(1)}) conditional(s32[]{:T(128)} %bitcast, (bf16[2,64,3584]{2,1,0:T(8,128)(2,1)}, f32[1,2,3584]{2,1,0:T(2,128)}, bf16[1,2,3584,256]{3,2,1,0:T(8,128)(2,1)}, bf16[1,2,3584,256]{3,2,1,0:T(8,128)(2,1)}, bf16[1,2,256,3584]{3,2,1,0:T(8,128)(2,1)}, ...), branch_computations={%region_0.0_spmd, %region_1.0_spmd, %region_2.0_spmd, %region_3.0_... | conditional | bytes 8 | solution.py:730
  7.5 208.3 %relay_layers.14 = bf16[1,2,64,3584]{3,2,1,0:T(8,128)(2,1)S(1)} custom-call(bf16[2,64,3584]{2,1,0:T(8,128)(2,1)} %get-tuple-element.224.tokens_hbm, f32[1,2,3584]{2,1,0:T(2,128)} %get-tuple-element.234.gain_ref, bf16[1,2,3584,256]{3,2,1,0:T(8,128)(2,1)} %get-tuple-element.236.gate_hbm, bf16[1,2,3584,256]{3,2,1,0:T(8,128)(2,1)} %get-tuple-element.238.up_hbm, ...), custom_call_target="tpu_custom_call" | custom-call | tf_op jit(solution)/shard_map/cond/branch_1_fun/relay_layers/pallas_call | solution.py:611
  216.3 0.9 copy.37
